TPU v7x, 256 devices: a whole 4x4x8 slice. The times are simulated.
256 devices in a mesh: comp: 64 (over z, x_lo, y), rank: 4 (over x_hi, core).
Axes of the slice: x: 4 (x_hi: 2, x_lo: 2; x = x_hi * 2 + x_lo), y: 4, z: 8, core: 2. Of those that a mesh axis runs over, the one named last changes fastest.
Arguments:
- density: float32 [256, 16384], P('comp'), may hold values from 0.1 to 1
- row_left: float32 [8, 256], replicated, may hold values from -4 to 4
- col_left: float32 [8, 16384], replicated, may hold values from -4 to 4
- row_right: float32 [8, 256], replicated, may hold values from -4 to 4
- col_right: float32 [8, 16384], replicated, may hold values from -4 to 4
Outputs:
- gain: float32 [256, 16384], P(('comp', 'rank'))
All inputs are finite; a program needn't handle non-finite values.
Results may differ from a plain program's by a relative error of at most 0.00021.
Values sent between devices are 32-bit elements; how exact they have to be, the bound alone decides.
A program may use at most 192 MiB of HBM per device.

v0:
```python
import math

import jax
import jax.numpy as jnp
from jax import lax
from jax.sharding import PartitionSpec as P

HIGHEST = lax.Precision.HIGHEST
direct_limit = 1024


def split_length(length):
    leading = math.isqrt(length)
    while length % leading != 0 or leading % 2 != 0 or length // leading % 2 != 0:
        leading += 1
    return (leading, length // leading)


def phase_table(rows_count, cols_count, length, direction):
    row_index = lax.broadcasted_iota(jnp.int32, (rows_count, cols_count), 0)
    col_index = lax.broadcasted_iota(jnp.int32, (rows_count, cols_count), 1)
    angles = (row_index * col_index % length).astype(jnp.float32) * (
        direction * 2.0 * math.pi / length
    )
    return (jnp.cos(angles), jnp.sin(angles))


def contract(pattern, first_operand, second_operand):
    return jnp.einsum(
        pattern,
        first_operand,
        second_operand,
        precision=HIGHEST,
        preferred_element_type=jnp.float32,
    )


def complex_contract(pattern, first_operand, second_operand, real_only):
    real_out = contract(pattern, first_operand[0], second_operand[0]) - contract(
        pattern, first_operand[1], second_operand[1]
    )
    if real_only:
        return (real_out, None)
    imag_out = contract(pattern, first_operand[0], second_operand[1]) + contract(
        pattern, first_operand[1], second_operand[0]
    )
    return (real_out, imag_out)


def direct_rows(signal, length, direction, half_in, half_out, real_only):
    in_count = length // 2 if half_in else length
    out_count = length // 2 if half_out else length
    table = phase_table(out_count, in_count, length, direction)
    result = complex_contract("kt,...tc->...kc", table, signal, real_only)
    return result


def transform(signal, length, direction, half_in, half_out, along_rows, real_only):
    if along_rows and length <= direct_limit:
        return direct_rows(signal, length, direction, half_in, half_out, real_only)
    leading, trailing = split_length(length)
    lead_in = leading // 2
    trail_out = trailing // 2 if half_out else trailing
    real_part, imag_part = signal
    outer_shape = real_part.shape[:-1]
    inner_shape = ()
    first_pattern = "kt,...ts->...ks"
    second_pattern = "...ks,sm->...mk"
    shape_in = outer_shape + (lead_in, trailing) + inner_shape
    shape_out = outer_shape + (trail_out * leading,) + inner_shape
    shaped = (real_part.reshape(shape_in), imag_part.reshape(shape_in))
    sectioned = complex_contract(
        first_pattern, phase_table(leading, lead_in, leading, direction), shaped, False
    )
    twist_real, twist_imag = phase_table(leading, trailing, length, direction)
    sectioned = (
        sectioned[0] * twist_real - sectioned[1] * twist_imag,
        sectioned[0] * twist_imag + sectioned[1] * twist_real,
    )
    result = complex_contract(
        second_pattern, sectioned, phase_table(trailing, trail_out, trailing, direction), real_only
    )
    if real_only:
        return result[0].reshape(shape_out)
    return (result[0].reshape(shape_out), result[1].reshape(shape_out))


def hermitian_split(spectrum, half_count):
    real_part, imag_part = spectrum
    mirror_real = jnp.concatenate(
        [real_part[..., :1], real_part[..., half_count + 1 :][..., ::-1]], axis=-1
    )
    mirror_imag = jnp.concatenate(
        [imag_part[..., :1], imag_part[..., half_count + 1 :][..., ::-1]], axis=-1
    )
    lower_real = real_part[..., :half_count]
    lower_imag = imag_part[..., :half_count]
    left_real = 0.5 * (lower_real + mirror_real)
    left_imag = 0.5 * (lower_imag - mirror_imag)
    right_real = 0.5 * (lower_imag + mirror_imag)
    right_imag = 0.5 * (mirror_real - lower_real)
    left_real = left_real.at[..., 0].set(real_part[..., 0])
    left_imag = left_imag.at[..., 0].set(real_part[..., half_count])
    right_real = right_real.at[..., 0].set(imag_part[..., 0])
    right_imag = right_imag.at[..., 0].set(imag_part[..., half_count])
    return jnp.stack([left_real, left_imag, right_real, right_imag])


def unpack_packed(real_part, imag_part):
    mirror_real = jnp.concatenate([real_part[..., :1], real_part[..., 1:][..., ::-1]], axis=-1)
    mirror_imag = jnp.concatenate([imag_part[..., :1], imag_part[..., 1:][..., ::-1]], axis=-1)
    zero_part = (0.5 * (real_part + mirror_real), 0.5 * (imag_part - mirror_imag))
    top_part = (0.5 * (imag_part + mirror_imag), 0.5 * (mirror_real - real_part))
    return (zero_part, top_part)


def body(density, row_left, col_left, row_right, col_right):
    rows_here, width = density.shape
    comp_count = lax.axis_size("comp")
    rank_count = lax.axis_size("rank")
    total_rows = rows_here * comp_count
    length_a = 2 * total_rows
    length_b = 2 * width
    comp_at = lax.axis_index("comp")
    rank_at = lax.axis_index("rank")
    rank_terms = row_left.shape[0]
    scaling = 0.5 / (length_a * length_b * math.sqrt(total_rows * width))
    term_count = rank_terms // rank_count
    term_start = rank_at * term_count
    row_start = comp_at * rows_here
    column_width = width // comp_count
    column_start = comp_at * column_width
    left_rows = lax.dynamic_slice(row_left, (term_start, row_start), (term_count, rows_here))
    right_rows = lax.dynamic_slice(row_right, (term_start, row_start), (term_count, rows_here))
    left_cols = lax.dynamic_slice_in_dim(col_left, term_start, term_count, 0)
    right_cols = lax.dynamic_slice_in_dim(col_right, term_start, term_count, 0)
    left_field = left_rows[:, :, None] * density[None] * left_cols[:, None, :]
    right_field = right_rows[:, :, None] * density[None] * right_cols[:, None, :]
    spectrum = transform((left_field, right_field), length_b, -1.0, True, False, False, False)
    outgoing = hermitian_split(spectrum, width)
    holds_zero = column_start == 0
    received = lax.all_to_all(outgoing, "comp", split_axis=3, concat_axis=2, tiled=True)
    left_a = transform((received[0], received[1]), length_a, -1.0, True, False, True, False)
    right_a = transform((received[2], received[3]), length_a, -1.0, True, False, True, False)
    prod_real = left_a[0] * right_a[0] - left_a[1] * right_a[1]
    prod_imag = left_a[0] * right_a[1] + left_a[1] * right_a[0]
    left_zero, left_top = unpack_packed(left_a[0][..., 0], left_a[1][..., 0])
    right_zero, right_top = unpack_packed(right_a[0][..., 0], right_a[1][..., 0])
    zero_real = left_zero[0] * right_zero[0] - left_zero[1] * right_zero[1]
    zero_imag = left_zero[0] * right_zero[1] + left_zero[1] * right_zero[0]
    top_real = left_top[0] * right_top[0] - left_top[1] * right_top[1]
    top_imag = left_top[0] * right_top[1] + left_top[1] * right_top[0]
    prod_real = prod_real.at[..., 0].set(
        jnp.where(holds_zero, zero_real - top_imag, prod_real[..., 0])
    )
    prod_imag = prod_imag.at[..., 0].set(
        jnp.where(holds_zero, zero_imag + top_real, prod_imag[..., 0])
    )
    products = jnp.stack([prod_real, prod_imag])
    summed = jnp.sum(products, axis=1)
    inverse_a = transform((summed[0], summed[1]), length_a, 1.0, False, True, True, False)
    stacked = jnp.stack([inverse_a[0], inverse_a[1]])
    returned = lax.all_to_all(stacked, "comp", split_axis=1, concat_axis=2, tiled=True)
    hb_real = returned[0]
    hb_imag = returned[1]
    nyquist = hb_imag[:, 0]
    coef_real = (2.0 * hb_real).at[:, 0].set(hb_real[:, 0])
    coef_imag = (2.0 * hb_imag).at[:, 0].set(0.0)
    values = transform((coef_real, coef_imag), length_b, 1.0, True, True, False, True)
    alternating = 1.0 - 2.0 * (lax.broadcasted_iota(jnp.int32, (1, width), 1) % 2).astype(
        jnp.float32
    )
    values = values + nyquist[:, None] * alternating
    gain_rows = lax.psum_scatter(values, "rank", scatter_dimension=0, tiled=True) * scaling
    return gain_rows


def solution(mesh):
    return jax.shard_map(
        body,
        mesh=mesh,
        in_specs=(P("comp", None), P(), P(), P(), P()),
        out_specs=P(("comp", "rank"), None),
        check_vma=False,
    )
```

profile of v0, /device:TPU:1, one launch (start us, length us, event | category | flops | bytes accessed | tf_op | source)
XLA Modules:
  0.0 694.7 jit_solution(15421583220333637120)
XLA Ops:
  7.5 1.3 dynamic-slice_bitcast_fusion
  9.0 1.0 copy.480
  10.1 0.8 dynamic_slice.12
  11.7 1.5 fusion.40
  13.2 1.5 fusion.39
  14.7 1.5 fusion.6
  16.1 1.5 fusion.5
  17.8 1.3 fusion.80
  19.1 2.3 fusion.4
  21.4 1.7 reshape.642
  23.2 1.2 slice.294
  24.3 1.5 fusion.79
  25.9 2.3 fusion.3
  28.1 1.7 reshape.643
  30.2 49.0 %reverse = f32[2,4,16384]{2,1,0:T(4,128)S(1)} reverse(f32[2,4,16384]{2,1,0:T(4,128)} %bitcast.270), dimensions={2} | reverse | bytes 1048576
  79.2 1.1 slice.361
  80.4 11.4 %reverse.1 = f32[2,4,16384]{2,1,0:T(4,128)S(1)} reverse(f32[2,4,16384]{2,1,0:T(4,128)S(1)} %bitcast.271), dimensions={2} | reverse | bytes 1048576
  92.2 2.2 multiply_bitcast_fusion.3
  95.2 1.3 scatter.31
  96.5 1.7 pad_maximum_fusion
  98.1 60.7 %copy.363 = f32[4,2,4,16384]{2,1,0,3:T(2,128)} copy(f32[4,2,4,16384]{3,2,1,0:T(4,128)S(1)} %pad_maximum_fusion) | data formatting | bytes 4194304 | tf_op jit(solution)/shard_map/stack | solution.py:106
  158.8 103.9 %reshape.658 = f32[64,1,8192]{2,1,0:T(1,128)} reshape(f32[16384,4,2,4]{3,2,1,0:T(2,128)} %bitcast.229) | data formatting | bytes 4194304
  262.7 13.6 %all-to-all-start = ((f32[64,1,8192]{2,1,0:T(1,128)}), f32[64,1,8192]{2,1,0:T(1,128)S(1)}, u32[]{:S(2)}, u32[]{:S(2)}) async-start(f32[64,1,8192]{2,1,0:T(1,128)} %reshape.658), calls=%async_computation | async-start | bytes 4194304 | tf_op jit(solution)/shard_map/all_to_all | solution.py:142
  276.3 48.4 %all-to-all-done = f32[64,1,8192]{2,1,0:T(1,128)S(1)} async-done(((f32[64,1,8192]{2,1,0:T(1,128)}), f32[64,1,8192]{2,1,0:T(1,128)S(1)}, u32[]{:S(2)}, u32[]{:S(2)}) %all-to-all-start) | async-done | bytes 2097184 | tf_op jit(solution)/shard_map/all_to_all | solution.py:142
  324.7 1.3 copy-done.2
  326.6 7.5 %reduce.22 = f32[64,8192]{1,0:T(8,128)S(1)} reduce(f32[64,1,8192]{2,1,0:T(1,128)} %copy-done.2, f32[]{:T(128)} %broadcast.549), dimensions={1}, to_apply=%all_to_all.22.reduce_sub_computation | reduce | bytes 4194308 | tf_op jit(solution)/shard_map/all_to_all | solution.py:142
  334.1 128.3 %reshape.659 = f32[16384,4,2,4]{3,2,1,0:T(2,128)} reshape(f32[64,8192]{1,0:T(8,128)S(1)} %reduce.22) | data formatting | bytes 4194304
  462.4 52.9 %copy.415 = f32[4,2,4,64,256]{4,3,2,1,0:T(8,128)S(1)} copy(f32[4,2,4,64,256]{2,1,0,4,3:T(2,128)} %bitcast.25) | data formatting | bytes 4194304 | tf_op jit(solution)/shard_map/all_to_all | solution.py:142
  515.3 1.0 fusion.265
  516.9 4.0 fusion.24
  520.9 1.4 copy.365
  522.6 4.0 fusion.28
  526.6 4.6 convolution_add_fusion.1
  531.2 0.8 copy.479
  532.7 4.0 fusion.26
  537.3 3.3 fusion.22
  540.6 4.4 fusion.1
  545.1 4.4 fusion.2
  549.5 4.4 multiply_subtract_fusion
  557.0 2.5 fusion.45
  559.6 2.5 fusion.46
  562.1 2.6 fusion.11
  564.7 2.6 fusion.10
  567.3 1.2 copy.394
  568.5 7.6 %all-to-all-start.1 = ((f32[2,256,256]{2,0,1:T(2,128)}), f32[2,256,256]{2,0,1:T(2,128)S(1)}, u32[]{:S(2)}, u32[]{:S(2)}) async-start(f32[2,256,256]{2,0,1:T(2,128)} %copy.394), calls=%async_computation.1 | async-start | bytes 1048576 | tf_op jit(solution)/shard_map/all_to_all | solution.py:163
  578.0 12.3 %all-to-all-done.1 = f32[2,256,256]{2,0,1:T(2,128)S(1)} async-done(((f32[2,256,256]{2,0,1:T(2,128)}), f32[2,256,256]{2,0,1:T(2,128)S(1)}, u32[]{:S(2)}, u32[]{:S(2)}) %all-to-all-start.1) | async-done | bytes 524320 | tf_op jit(solution)/shard_map/all_to_all | solution.py:163
  590.8 4.6 copy.395
  595.4 3.8 broadcast_multiply_fusion.1
  599.2 3.2 copy-done
  602.4 1.3 broadcast_select_fusion.3
  603.7 1.3 scatter.36
  605.0 6.6 copy.396
  611.5 1.1 fusion.87
  612.6 4.6 copy.397
  617.2 3.8 broadcast_multiply_fusion
  621.0 3.2 copy-done.1
  624.9 1.3 scatter.39
  626.2 6.6 copy.398
  632.8 1.1 fusion.85
  633.8 1.1 fusion.8
  634.9 1.1 fusion.7
  638.1 0.9 multiply_add_fusion.2
  639.6 45.8 %all-reduce.3.cloned.1.call-done = f32[4,16384]{1,0:T(4,128)} async-done(((f32[4,16384]{1,0:T(4,128)}), f32[4,16384]{1,0:T(4,128)}) %all-reduce.3.cloned.1.call-update) | async-done | bytes 262160
  685.4 2.3 dynamic-slice_multiply_fusion
  (80 shorter events, 15.0 us)
Async XLA Ops:
  94.4 0.8 copy-start.3
  262.7 62.0 %all-to-all-start = ((f32[64,1,8192]{2,1,0:T(1,128)}), f32[64,1,8192]{2,1,0:T(1,128)S(1)}, u32[]{:S(2)}, u32[]{:S(2)}) async-start(f32[64,1,8192]{2,1,0:T(1,128)} %reshape.658), calls=%async_computation | async-start | bytes 4194304 | tf_op jit(solution)/shard_map/all_to_all | solution.py:142
  324.7 1.3 copy-start.2
  532.6 4.0 copy-start.4
  568.5 21.9 %all-to-all-start.1 = ((f32[2,256,256]{2,0,1:T(2,128)}), f32[2,256,256]{2,0,1:T(2,128)S(1)}, u32[]{:S(2)}, u32[]{:S(2)}) async-start(f32[2,256,256]{2,0,1:T(2,128)} %copy.394), calls=%async_computation.1 | async-start | bytes 1048576 | tf_op jit(solution)/shard_map/all_to_all | solution.py:163
  576.1 109.2 %all-reduce.3.cloned.1.call-start = ((), (), s32[]{:S(2)}) async-start(), calls=%async_computation.2 | async-start | bytes 524288
  599.2 3.2 copy-start
  621.0 3.2 copy-start.1
  626.2 12.8 %copy-start.5 = (u32[256]{0:T(256)S(1)}, u32[256]{0:T(256)}, u32[]{:S(2)}) copy-start(u32[256]{0:T(256)} %constant.325) | copy-start | bytes 3076
Sparse Core Ops, SparseCore 0:
  639.1 46.2 all-reduce.2
where the time goes:
time: 707 us; the launch traced here: 695 us
  local copies, waits for them, and re-layouts  463 us (65%)
  waiting for transfers between devices  107 us (15%)
  matrix products  62.1 us (9%)
  other arithmetic  27.5 us (4%)
  starting transfers between devices  21.3 us (3%)
  between operations  14.2 us (2%)
    unnamed x31, local copies, waits for them, and re-layouts  307 us
    dot_general x26, matrix products, contract(): jnp.einsum(pattern, first_operand, second_operand, precision=HIGHEST, pre...  62.1 us
    another operation x3, local copies, waits for them, and re-layouts, hermitian_split(): return jnp.stack([left_real, left_imag, right_real, right_imag])  60.7 us
    all_to_all x2, local copies, waits for them, and re-layouts, body(): lax.all_to_all(outgoing, 'comp', split_axis=3, concat_axis=2, tiled=True)  53.4 us
    all_to_all x1, waiting for transfers between devices, body(): lax.all_to_all(outgoing, 'comp', split_axis=3, concat_axis=2, tiled=True)  48.4 us
    unnamed x2, waiting for transfers between devices  45.8 us
  transfers between devices with their start and end apart: 3, of which 3 were waited for; matrix products, arithmetic and copies ran while one was open for 0% of the time, Pallas kernels for 0%

commit v1 on v0

v1 whole, which is shorter than its diff:
```python
import functools
import math

import jax
import jax.numpy as jnp
import ml_dtypes
import numpy as np
from jax import lax
from jax.experimental import pallas as pl
from jax.experimental.pallas import tpu as pltpu
from jax.sharding import PartitionSpec as P

MESH = pl.DeviceIdType.MESH
BF16 = jnp.bfloat16
F32 = jnp.float32
SIZE = {"x": 4, "y": 4, "z": 8}


def halves(table):
    table = np.asarray(table, np.float64)
    high = table.astype(ml_dtypes.bfloat16)
    low = (table - high.astype(np.float64)).astype(ml_dtypes.bfloat16)
    return np.stack([high, low])


def phase(numerator, length, sign):
    angle = sign * 2.0 * np.pi * (np.asarray(numerator) % length) / length
    return np.cos(angle), np.sin(angle)


def as_real(cos, sin):
    return np.block([[cos, -sin], [sin, cos]])


def tables():
    k1, t1 = np.arange(256)[:, None], np.arange(128)[None, :]
    k2, s = np.arange(128)[:, None], np.arange(128)[None, :]
    lead = as_real(*phase(k1 * t1, 256, -1))
    twist = np.stack(phase(k1 * s, 32768, -1)).astype(np.float32)
    trail = as_real(*phase(k2 * s, 128, -1)).T
    back_trail = as_real(*phase(k2 * s, 128, 1)).T
    back_lead = as_real(*phase(np.arange(128)[:, None] * np.arange(256)[None, :], 256, 1))
    order = [2 * c + t + 128 * part for c in range(64) for part in (0, 1) for t in (0, 1)]
    back_lead = back_lead[np.array(order)]
    return halves(lead), twist, halves(trail), halves(back_trail), halves(back_lead)


def final_tables(total):
    grid = np.arange(64)
    cos, sin = phase(grid[:, None] * grid[None, :], 64, 1)
    full = as_real(cos, sin)
    order = [4 * sub + q + 64 * part for q in range(4) for part in (0, 1) for sub in range(16)]
    rows = full[np.array(order)]
    scale = 0.5 / (math.sqrt(total) * 256.0 * 32768.0)
    mix = np.zeros((4, 64, 4, 2, 16))
    for q in range(4):
        for c in range(64):
            a = 4 * c + q
            for r in range(4):
                cc, ss = phase(a * (4 * r + 1), 1024, 1)
                mix[q, c, r, 0, c % 16] = cc * scale
                mix[q, c, r, 1, c % 16] = -ss * scale
    return halves(rows), halves(mix.reshape(4, 64, 128))


def split(value):
    high = value.astype(BF16)
    return high, (value - high.astype(F32)).astype(BF16)


def dot3(first, second):
    dot = functools.partial(jnp.dot, preferred_element_type=F32)
    return dot(first[0], second[0]) + (dot(first[0], second[1]) + dot(first[1], second[0]))


def place():
    comp, rank = lax.axis_index("comp"), lax.axis_index("rank")
    return {"z": comp // 8, "y": comp % 4, "x": rank // 2 * 2 + comp // 4 % 2, "core": rank % 2}


def device(at):
    return {"comp": (at["z"] * 2 + at["x"] % 2) * 4 + at["y"], "rank": at["x"] // 2 * 2 + at["core"]}


PARTS = ((("x", "y", "z"), 0, 20), (("y", "z", "x"), 20, 22), (("z", "x", "y"), 42, 22))


def gather_kernel(d_ref, out_ref, local_sem, send_sem, recv_sem):
    me = place()

    def neighbour(axis, offset):
        return device({**me, axis: (me[axis] + offset) % SIZE[axis]})

    local = pltpu.make_async_copy(
        d_ref.at[pl.ds(me["core"] * 64, 64), pl.ds(me["x"] // 2 * 2, 2)],
        out_ref.at[me["z"], me["y"], me["x"]],
        local_sem,
    )
    local.start()
    barrier = pltpu.get_barrier_semaphore()
    peers = [("x", 1), ("x", 2), ("x", 3), ("y", 1), ("y", 2), ("y", 3), ("z", 1), ("z", -1)]
    for axis, offset in peers:
        pl.semaphore_signal(barrier, inc=1, device_id=neighbour(axis, offset), device_id_type=MESH)
    pl.semaphore_wait(barrier, len(peers))
    local.wait()
    started = []

    def send(block, axis, offset):
        i = len(started)
        copy = pltpu.make_async_remote_copy(
            src_ref=block,
            dst_ref=block,
            send_sem=send_sem.at[i],
            recv_sem=recv_sem.at[i],
            device_id=neighbour(axis, offset),
            device_id_type=MESH,
        )
        copy.start()
        started.append(copy)
        return copy

    def view(done, axis, index, low, count, half=None):
        where = []
        for name in ("z", "y", "x"):
            if name == axis:
                where.append(index % SIZE[name])
            elif name in done:
                if half is not None and name == done[-1]:
                    where.append(pl.ds(half * SIZE[name] // 2, SIZE[name] // 2))
                else:
                    where.append(pl.ds(0, SIZE[name]))
            else:
                where.append(me[name])
        return out_ref.at[tuple(where) + (pl.ds(low, count),)]

    def ring(done, axis, low, count):
        steps = SIZE[axis] // 2
        right = left = None
        for step in range(1, steps + 1):
            half = (0, 1) if done and step == steps else (None, None)
            if right is not None:
                right.wait_recv()
            right = send(view(done, axis, me[axis] - (step - 1), low, count, half[0]), axis, 1)
            if left is not None:
                left.wait_recv()
                left = None
            if done or step < steps:
                left = send(view(done, axis, me[axis] + (step - 1), low, count, half[1]), axis, -1)
            yield
        right.wait_recv()
        if left is not None:
            left.wait_recv()

    def direct(axis, low, count):
        copies = [send(view((), axis, me[axis], low, count), axis, o) for o in range(1, SIZE[axis])]
        yield
        for copy in copies:
            copy.wait_recv()

    def part(order, low, count):
        first, second, third = order
        yield from ring((), first, low, count) if first == "z" else direct(first, low, count)
        yield from ring((first,), second, low, count)
        yield from ring((first, second), third, low, count)

    live = [part(*p) for p in PARTS]
    while live:
        for one in list(live):
            if next(one, 0) == 0:
                live.remove(one)
    for copy in started:
        copy.wait_send()


def gather(density):
    return pl.pallas_call(
        gather_kernel,
        out_shape=jax.ShapeDtypeStruct((8, 4, 4, 64, 2, 128), F32),
        in_specs=[pl.BlockSpec(memory_space=pl.ANY)],
        out_specs=pl.BlockSpec(memory_space=pl.ANY),
        scratch_shapes=[
            pltpu.SemaphoreType.DMA,
            pltpu.SemaphoreType.DMA((64,)),
            pltpu.SemaphoreType.DMA((64,)),
        ],
        compiler_params=pltpu.CompilerParams(collective_id=0, has_side_effects=True),
    )(density)


def rows_kernel(core_ref, d_ref, w_ref, left_ref, right_ref, own_ref, other_ref):
    weights = (w_ref[0], w_ref[1])
    source = d_ref.reshape(128 * 16, 128)
    own_rows = own_ref.reshape(32 * 8, 128)
    other_rows = other_ref.reshape(32 * 8, 128)
    for t in range(8):
        x = jnp.concatenate(
            [source[pl.ds(2 * t + p, 128, stride=16), :] for p in (0, 1)], axis=0
        )
        field = dot3(weights, split(x))
        cols = jnp.concatenate(
            [left_ref[:, t * 128 : (t + 1) * 128], right_ref[:, t * 128 : (t + 1) * 128]], axis=0
        )
        field = field * jnp.concatenate([cols] * 4, axis=0)
        own_rows[pl.ds(t, 32, stride=8), :] = field[:32]
        other_rows[pl.ds(t, 32, stride=8), :] = field[32:]


def rows(core, gathered, weights, col_left, col_right):
    out = jax.ShapeDtypeStruct((32, 64, 128), F32)
    return pl.pallas_call(
        rows_kernel,
        out_shape=(out, out),
        grid_spec=pltpu.PrefetchScalarGridSpec(
            num_scalar_prefetch=1,
            grid=(8,),
            in_specs=[
                pl.BlockSpec((128, 16, 128), lambda i, core: (0, i, 0)),
                pl.BlockSpec((2, 64, 256), lambda i, core: (0, 0, 0)),
                pl.BlockSpec((8, 1024), lambda i, core: (0, core[0] * 8 + i)),
                pl.BlockSpec((8, 1024), lambda i, core: (0, core[0] * 8 + i)),
            ],
            out_specs=[pl.BlockSpec((32, 8, 128), lambda i, core: (0, i, 0))] * 2,
        ),
        compiler_params=pltpu.CompilerParams(vmem_limit_bytes=40 << 20),
    )(core, gathered, weights, col_left, col_right)


def columns_kernel(core_ref, own_ref, got_ref, lead_ref, twist_ref, trail_ref, back_trail_ref, back_lead_ref, out_ref, sum_ref):
    step = pl.program_id(0)
    first = core_ref[0] == 0

    def loaded(part, side):
        own, got = own_ref[part, side, 0], got_ref[part, side, 0]
        return jnp.concatenate([jnp.where(first, own, got), jnp.where(first, got, own)], axis=0)

    def table(ref):
        return ref[0], ref[1]

    x = jnp.concatenate(
        [jnp.concatenate([loaded(part, side) for side in (0, 1)], axis=1) for part in (0, 1)], axis=0
    )
    y = dot3(table(lead_ref), split(x))
    spectra = []
    for side in (0, 1):
        real, imag = y[:256, side * 128 : side * 128 + 128], y[256:, side * 128 : side * 128 + 128]
        cos, sin = twist_ref[0], twist_ref[1]
        turned = jnp.concatenate([real * cos - imag * sin, real * sin + imag * cos], axis=1)
        spectra.append(dot3(split(turned), table(trail_ref)))
    left, right = spectra
    lr, li, rr, ri = left[:, :128], left[:, 128:], right[:, :128], right[:, 128:]
    product = jnp.concatenate([lr * rr - li * ri, lr * ri + li * rr], axis=1)

    @pl.when(step == 0)
    def _():
        sum_ref[...] = product

    @pl.when(step > 0)
    def _():
        sum_ref[...] += product

    @pl.when(step == pl.num_programs(0) - 1)
    def _():
        back = dot3(split(sum_ref[...]), table(back_trail_ref))
        real, imag = back[:, :128], back[:, 128:]
        cos, sin = twist_ref[0], twist_ref[1]
        turned = jnp.concatenate([real * cos + imag * sin, imag * cos - real * sin], axis=0)
        out_ref[...] = dot3(table(back_lead_ref), split(turned))


def columns(core, own, got):
    lead, twist, trail, back_trail, back_lead = tables()

    def whole(array):
        return pl.BlockSpec(array.shape, lambda r, core: (0,) * array.ndim)

    constants = (lead, twist, trail, back_trail, back_lead)
    return pl.pallas_call(
        columns_kernel,
        out_shape=jax.ShapeDtypeStruct((256, 128), F32),
        grid_spec=pltpu.PrefetchScalarGridSpec(
            num_scalar_prefetch=1,
            grid=(8,),
            in_specs=[pl.BlockSpec((2, 2, 1, 64, 128), lambda r, core: (0, 0, r, 0, 0))] * 2
            + [whole(c) for c in constants],
            out_specs=pl.BlockSpec((256, 128), lambda r, core: (0, 0)),
            scratch_shapes=[pltpu.VMEM((256, 256), F32)],
        ),
        compiler_params=pltpu.CompilerParams(vmem_limit_bytes=40 << 20),
    )(core, own.reshape(2, 2, 8, 64, 128), got.reshape(2, 2, 8, 64, 128), *(jnp.asarray(c) for c in constants))


def finish_kernel(q_ref, rows_ref, mix_ref, out_ref, got_ref, part_ref, all_ref, line_ref, sems):
    comp, rank = lax.axis_index("comp"), lax.axis_index("rank")

    def peer(offset):
        return {"comp": (comp + offset) % 64, "rank": rank}

    def other(offset):
        return {"comp": comp, "rank": (rank + offset) % 4}

    barrier = pltpu.get_barrier_semaphore()

    def greet(i, carry):
        pl.semaphore_signal(barrier, inc=1, device_id=peer(i), device_id_type=MESH)
        return carry

    lax.fori_loop(1, 64, greet, 0)
    for i in range(1, 4):
        pl.semaphore_signal(barrier, inc=1, device_id=other(i), device_id_type=MESH)
    pl.semaphore_wait(barrier, 66)

    def exchange(source, target, send_sem, recv_sem):
        own = pltpu.make_async_copy(source.at[comp], target.at[comp], recv_sem)
        own.start()

        def send(i, carry):
            to = peer(i)
            pltpu.make_async_remote_copy(
                src_ref=source.at[to["comp"]],
                dst_ref=target.at[comp],
                send_sem=send_sem,
                recv_sem=recv_sem,
                device_id=to,
                device_id_type=MESH,
            ).start()
            return carry

        lax.fori_loop(1, 64, send, 0)
        pltpu.make_async_copy(source, target, recv_sem).wait()
        rest = pl.ds(0, 63)
        pltpu.make_async_copy(source.at[rest], target.at[rest], send_sem).wait()

    exchange(q_ref, got_ref, sems.at[0], sems.at[1])
    x = jnp.concatenate(
        [
            jnp.concatenate([got_ref[:, 2 * part + t, :] for t in (0, 1)], axis=1)
            for part in (0, 1)
        ],
        axis=0,
    )
    part = dot3((rows_ref[0], rows_ref[1]), split(x))
    for q in range(4):
        part_ref[q] = part[32 * q : 32 * q + 32]
    own = pltpu.make_async_copy(part_ref.at[rank], all_ref.at[rank], sems.at[2])
    own.start()
    copies = []
    for i in range(1, 4):
        to = other(i)
        copy = pltpu.make_async_remote_copy(
            src_ref=part_ref.at[to["rank"]],
            dst_ref=all_ref.at[rank],
            send_sem=sems.at[3 + i],
            recv_sem=sems.at[6 + i],
            device_id=to,
            device_id_type=MESH,
        )
        copy.start()
        copies.append(copy)
    own.wait()
    for copy in copies:
        copy.wait()
    lines = dot3((mix_ref[0, rank], mix_ref[1, rank]), split(all_ref[...].reshape(128, 256)))
    for t in (0, 1):
        line_ref[:, t, :] = lines[:, t * 128 : t * 128 + 128]
    exchange(line_ref, out_ref, sems.at[3], sems.at[10])


def finish(q, total):
    rows_table, mix = final_tables(total)
    vmem = pl.BlockSpec(memory_space=pltpu.VMEM)
    return pl.pallas_call(
        finish_kernel,
        out_shape=jax.ShapeDtypeStruct((64, 2, 128), F32),
        in_specs=[vmem] * 3,
        out_specs=vmem,
        scratch_shapes=[
            pltpu.VMEM((64, 4, 128), F32),
            pltpu.VMEM((4, 32, 256), F32),
            pltpu.VMEM((4, 32, 256), F32),
            pltpu.VMEM((64, 2, 128), F32),
            pltpu.SemaphoreType.DMA((11,)),
        ],
        compiler_params=pltpu.CompilerParams(
            collective_id=1, has_side_effects=True, vmem_limit_bytes=40 << 20
        ),
    )(q.reshape(64, 4, 128), jnp.asarray(rows_table), jnp.asarray(mix))


def row_weights(row_left, row_right):
    comp, rank = lax.axis_index("comp"), lax.axis_index("rank")
    first = 4 * comp + rank
    second = 4 * comp + (rank // 2 * 2 + 1 - rank % 2)
    parity = np.arange(2)[:, None]
    chip = np.arange(128)[None, :]
    z, y, x = chip // 16, chip // 4 % 4, chip % 4
    a = (4 * ((z * 2 + x % 2) * 4 + y) + x // 2 * 2 + parity).reshape(-1)
    perm = jnp.asarray(a, jnp.int32)
    both = jnp.concatenate([row_left, row_right], axis=0)
    both = both.reshape(16, 8, 2, 4, 2, 2).transpose(0, 5, 1, 3, 4, 2).reshape(16, 256)
    frequency = jnp.stack([first, second])
    angle = (perm[None, :] * (4 * frequency[:, None] + 1) % 1024).astype(F32) * (-2.0 * math.pi / 1024)
    turn = jnp.stack([jnp.cos(angle), jnp.sin(angle)], axis=1)
    weights = (turn[:, :, None, :] * both[None, None]).reshape(64, 256)
    high = lax.reduce_precision(weights, 8, 7)
    return jnp.stack([high.astype(BF16), (weights - high).astype(BF16)])


def body(density, row_left, col_left, row_right, col_right):
    core = (lax.axis_index("rank") % 2).astype(jnp.int32).reshape(1)
    weights = row_weights(row_left, row_right)
    gathered = gather(density.reshape(4, 128, 128).transpose(1, 0, 2))
    own, other = rows(core, gathered.reshape(128, 128, 128), weights, col_left, col_right)
    got = lax.ppermute(other, "rank", [(0, 1), (1, 0), (2, 3), (3, 2)])
    q = columns(core, own, got)
    return finish(q, 256 * 16384).reshape(1, 16384)


def solution(mesh):
    return jax.shard_map(
        body,
        mesh=mesh,
        in_specs=(P("comp", None), P(), P(), P(), P()),
        out_specs=P(("comp", "rank"), None),
        check_vma=False,
    )
```

time: 707 us -> 132 us (0.19); the launches traced: 695 us -> 132 us
  local copies, waits for them, and re-layouts: 463 us -> 4.32 us
  Pallas kernels: 0 us -> 113 us
  waiting for transfers between devices: 107 us -> 2.29 us
  matrix products: 62.1 us -> 0 us
  other arithmetic: 27.5 us -> 1.76 us
  between operations: 14.2 us -> 0.18 us
  starting transfers between devices: 21.3 us -> 10.6 us
    unnamed x31 -> x21, local copies, waits for them, and re-layouts: 307 us -> 4.09 us
    pallas_call x0 -> x4, Pallas kernels: none -> 113 us  [the longest x1 74 us: gather(): pl.pallas_call(gather_kernel, out_shape=jax.ShapeDtypeStruct((8, 4, 4, 64...]
    dot_general x26 -> x0, matrix products: 62.1 us -> none  [contract(): jnp.einsum(pattern, first_operand, second_operand, precision=HIGHEST, pre...]
    another operation x4 -> x0, local copies, waits for them, and re-layouts: 61.9 us -> none  [the longest x3 60.7 us: hermitian_split(): return jnp.stack([left_real, left_imag, right_real, right_imag])]
    all_to_all x2 -> x0, waiting for transfers between devices: 60.7 us -> none  [the longest x1 48.4 us: body(): lax.all_to_all(outgoing, 'comp', split_axis=3, concat_axis=2, tiled=True)]
    all_to_all x2 -> x0, local copies, waits for them, and re-layouts: 53.4 us -> none  [body(): lax.all_to_all(outgoing, 'comp', split_axis=3, concat_axis=2, tiled=True)]
    unnamed x2 -> x0, waiting for transfers between devices: 45.8 us -> none
    all_to_all x2 -> x0, starting transfers between devices: 21.2 us -> none  [the longest x1 13.6 us: body(): lax.all_to_all(outgoing, 'comp', split_axis=3, concat_axis=2, tiled=True)]
  transfers between devices with their start and end apart: 3 -> 1, of which waited for: 3 -> 1; matrix products, arithmetic and copies ran while one was open for 0% -> 0% of each run, Pallas kernels for 0% -> 0%
where the time goes in v1:
time: 132 us
  Pallas kernels  113 us (86%)
  starting transfers between devices  10.6 us (8%)
  local copies, waits for them, and re-layouts  4.32 us (3%)
  waiting for transfers between devices  2.29 us (2%)
  other arithmetic  1.76 us (1%)
    pallas_call x1, Pallas kernels, gather(): pl.pallas_call(gather_kernel, out_shape=jax.ShapeDtypeStruct((8, 4, 4, 64...  74 us
    pallas_call x1, Pallas kernels, finish(): pl.pallas_call(finish_kernel, out_shape=jax.ShapeDtypeStruct((64, 2, 128)...  24.4 us
    ppermute x1, starting transfers between devices, body(): got = lax.ppermute(other, 'rank', [(0, 1), (1, 0), (2, 3), (3, 2)])  10.6 us
    pallas_call x1, Pallas kernels, columns(): pl.pallas_call(columns_kernel, out_shape=jax.ShapeDtypeStruct((256, 128),...  9.53 us
    pallas_call x1, Pallas kernels, rows(): pl.pallas_call(rows_kernel, out_shape=(out, out), grid_spec=pltpu.Prefetc...  5.14 us
    unnamed x21, local copies, waits for them, and re-layouts  4.09 us
  transfers between devices with their start and end apart: 1, of which 1 were waited for; matrix products, arithmetic and copies ran while one was open for 0% of the time, Pallas kernels for 0%

profile of v1, /device:TPU:1, one launch (start us, length us, event | category | flops | bytes accessed | tf_op | source)
XLA Modules:
  0.0 132.2 jit_solution(9093358133057032432)
XLA Ops:
  0.0 0.0 copy-start.2
  0.0 0.0 copy-start.1
  0.0 0.8 pad_maximum_fusion.1
  0.8 0.1 copy.18
  0.9 0.1 copy.19
  1.0 0.1 copy.20
  1.0 0.1 fusion.4
  1.1 0.8 fusion.6
  2.0 0.0 copy-start.3
  2.0 0.0 copy-start.4
  2.0 0.0 copy-start.5
  2.1 0.0 copy-start.6
  2.1 0.0 copy-start.7
  2.1 0.0 copy-start.9
  2.1 74.0 %shard_map.127 = f32[8,4,4,64,2,128]{5,4,3,2,1,0:T(2,128)} custom-call(f32[128,4,128]{2,1,0:T(4,128)} %bitcast.23), custom_call_target="tpu_custom_call" | custom-call | tf_op jit(solution)/shard_map/pallas_call | solution.py:176
  76.1 0.0 copy-start.8
  76.1 0.0 copy-done.2
  76.1 0.0 copy-done.1
  76.1 0.0 copy-start
  76.1 3.4 %copy-done = f32[8,4,4,64,2,128]{5,4,3,2,1,0:T(2,128)S(1)} copy-done((f32[8,4,4,64,2,128]{5,4,3,2,1,0:T(2,128)S(1)}, f32[8,4,4,64,2,128]{5,4,3,2,1,0:T(2,128)}, u32[]{:S(2)}) %copy-start) | copy-done | bytes 8388632
  79.5 5.1 %shard_map.128 = (f32[32,64,128]{2,1,0:T(8,128)S(1)}, f32[32,64,128]{2,1,0:T(8,128)S(1)}) custom-call(s32[1]{0:T(128)} %bitcast.core_ref, f32[128,128,128]{2,1,0:T(8,128)S(1)} %bitcast.16, bf16[2,64,256]{2,1,0:T(8,128)(2,1)S(1)} %pad_maximum_fusion.w_ref, f32[8,16384]{1,0:T(8,128)S(1)} %copy-done.1, f32[8,16384]{1,0:T(8,128)S(1)} %copy-done.2), custom_call_target="tpu_custom_call" | custom-call | tf_op jit(solution)/shard_map/pallas_call | solution.py:210
  84.7 10.6 %collective-permute-start = (f32[32,64,128]{2,1,0:T(8,128)S(1)}, f32[32,64,128]{2,1,0:T(8,128)S(1)}, u32[]{:S(2)}, u32[]{:S(2)}) collective-permute-start(f32[32,64,128]{2,1,0:T(8,128)S(1)} %get-tuple-element.8), channel_id=1, source_target_pairs={{0,1},{1,0},{2,3},{3,2},{4,5},{5,4},{6,7},{7,6},{8,9},{9,8},{10,11... | collective-permute-start | bytes 3145736 | tf_op jit(solution)/shard_map/ppermute | solution.py:413
  95.3 2.3 %collective-permute-done = f32[32,64,128]{2,1,0:T(8,128)S(1)} collective-permute-done((f32[32,64,128]{2,1,0:T(8,128)S(1)}, f32[32,64,128]{2,1,0:T(8,128)S(1)}, u32[]{:S(2)}, u32[]{:S(2)}) %collective-permute-start) | collective-permute-done | bytes 1048608 | tf_op jit(solution)/shard_map/ppermute | solution.py:413
  97.6 0.0 copy-done.3
  97.6 0.0 copy-done.4
  97.6 0.0 copy-done.5
  97.6 0.0 copy-done.6
  97.6 0.0 copy-done.7
  97.6 9.5 %shard_map.129 = f32[256,128]{1,0:T(8,128)S(1)} custom-call(s32[1]{0:T(128)} %bitcast.core_ref, f32[2,2,8,64,128]{4,3,2,1,0:T(8,128)S(1)} %bitcast.17, f32[2,2,8,64,128]{4,3,2,1,0:T(8,128)S(1)} %bitcast.18, bf16[2,512,256]{2,1,0:T(8,128)(2,1)S(1)} %copy-done.4, f32[2,256,128]{2,1,0:T(8,128)S(1)} %copy-done.7, bf16[2,256,256]{2,1,0:T(8,128)(2,1)S(1)} %copy-done.6, ...), custom_call_target="tpu_custom_call" | custom-call | tf_op jit(solution)/shard_map/pallas_call | solution.py:277
  107.1 0.0 copy-done.9
  107.1 0.0 copy-done.8
  107.1 24.4 %shard_map.130 = f32[64,2,128]{2,1,0:T(2,128)S(1)} custom-call(f32[64,4,128]{2,1,0:T(4,128)S(1)} %bitcast.19, bf16[2,128,128]{2,1,0:T(8,128)(2,1)S(1)} %copy-done.9, bf16[2,4,64,128]{3,2,1,0:T(8,128)(2,1)S(1)} %copy-done.8), custom_call_target="tpu_custom_call" | custom-call | tf_op jit(solution)/shard_map/pallas_call | solution.py:371
  131.6 0.6 copy.22
  (4 shorter events, 0.0 us)
Async XLA Ops:
  0.0 76.1 %copy-start.2 = (f32[8,16384]{1,0:T(8,128)S(1)}, f32[8,16384]{1,0:T(8,128)}, u32[]{:S(2)}) copy-start(f32[8,16384]{1,0:T(8,128)} %right_ref.1) | copy-start | bytes 1572868
  0.0 76.1 %copy-start.1 = (f32[8,16384]{1,0:T(8,128)S(1)}, f32[8,16384]{1,0:T(8,128)}, u32[]{:S(2)}) copy-start(f32[8,16384]{1,0:T(8,128)} %left_ref.1) | copy-start | bytes 1572868
  2.0 95.5 %copy-start.3 = (bf16[2,256,512]{2,1,0:T(8,128)(2,1)S(1)}, bf16[2,256,512]{2,1,0:T(8,128)(2,1)}, u32[]{:S(2)}) copy-start(bf16[2,256,512]{2,1,0:T(8,128)(2,1)} %constant.77.clone.back_lead_ref) | copy-start | bytes 1572868
  2.0 95.5 %copy-start.4 = (bf16[2,512,256]{2,1,0:T(8,128)(2,1)S(1)}, bf16[2,512,256]{2,1,0:T(8,128)(2,1)}, u32[]{:S(2)}) copy-start(bf16[2,512,256]{2,1,0:T(8,128)(2,1)} %constant.73.clone.lead_ref) | copy-start | bytes 1572868
  2.0 95.5 %copy-start.5 = (bf16[2,256,256]{2,1,0:T(8,128)(2,1)S(1)}, bf16[2,256,256]{2,1,0:T(8,128)(2,1)}, u32[]{:S(2)}) copy-start(bf16[2,256,256]{2,1,0:T(8,128)(2,1)} %constant.76.clone.back_trail_ref) | copy-start | bytes 786436
  2.1 95.5 %copy-start.6 = (bf16[2,256,256]{2,1,0:T(8,128)(2,1)S(1)}, bf16[2,256,256]{2,1,0:T(8,128)(2,1)}, u32[]{:S(2)}) copy-start(bf16[2,256,256]{2,1,0:T(8,128)(2,1)} %constant.75.clone.trail_ref) | copy-start | bytes 786436
  2.1 95.5 %copy-start.7 = (f32[2,256,128]{2,1,0:T(8,128)S(1)}, f32[2,256,128]{2,1,0:T(8,128)}, u32[]{:S(2)}) copy-start(f32[2,256,128]{2,1,0:T(8,128)} %constant.74.clone.twist_ref) | copy-start | bytes 786436
  2.1 105.0 %copy-start.9 = (bf16[2,128,128]{2,1,0:T(8,128)(2,1)S(1)}, bf16[2,128,128]{2,1,0:T(8,128)(2,1)}, u32[]{:S(2)}) copy-start(bf16[2,128,128]{2,1,0:T(8,128)(2,1)} %constant.78.clone.rows_ref) | copy-start | bytes 196612
  76.1 31.0 %copy-start.8 = (bf16[2,4,64,128]{3,2,1,0:T(8,128)(2,1)S(1)}, bf16[2,4,64,128]{3,2,1,0:T(8,128)(2,1)}, u32[]{:S(2)}) copy-start(bf16[2,4,64,128]{3,2,1,0:T(8,128)(2,1)} %constant.79.clone.mix_ref) | copy-start | bytes 393220
  76.1 3.4 %copy-start = (f32[8,4,4,64,2,128]{5,4,3,2,1,0:T(2,128)S(1)}, f32[8,4,4,64,2,128]{5,4,3,2,1,0:T(2,128)}, u32[]{:S(2)}) copy-start(f32[8,4,4,64,2,128]{5,4,3,2,1,0:T(2,128)} %shard_map.127) | copy-start | bytes 25165828
  84.7 12.9 %collective-permute-start = (f32[32,64,128]{2,1,0:T(8,128)S(1)}, f32[32,64,128]{2,1,0:T(8,128)S(1)}, u32[]{:S(2)}, u32[]{:S(2)}) collective-permute-start(f32[32,64,128]{2,1,0:T(8,128)S(1)} %get-tuple-element.8), channel_id=1, source_target_pairs={{0,1},{1,0},{2,3},{3,2},{4,5},{5,4},{6,7},{7,6},{8,9},{9,8},{10,11... | collective-permute-start | bytes 3145736 | tf_op jit(solution)/shard_map/ppermute | solution.py:413

commit v2 on v1

v2 whole, which is shorter than its diff:
```python
import functools
import math

import jax
import jax.numpy as jnp
import ml_dtypes
import numpy as np
from jax import lax
from jax.experimental import pallas as pl
from jax.experimental.pallas import tpu as pltpu
from jax.sharding import PartitionSpec as P

MESH = pl.DeviceIdType.MESH
BF16 = jnp.bfloat16
F32 = jnp.float32
SIZE = {"x": 4, "y": 4, "z": 8}


def halves(table):
    table = np.asarray(table, np.float64)
    high = table.astype(ml_dtypes.bfloat16)
    low = (table - high.astype(np.float64)).astype(ml_dtypes.bfloat16)
    return np.stack([high, low])


def phase(numerator, length, sign):
    angle = sign * 2.0 * np.pi * (np.asarray(numerator) % length) / length
    return np.cos(angle), np.sin(angle)


def as_real(cos, sin):
    return np.block([[cos, -sin], [sin, cos]])


def tables():
    k1, t1 = np.arange(256)[:, None], np.arange(128)[None, :]
    k2, s = np.arange(128)[:, None], np.arange(128)[None, :]
    lead = as_real(*phase(k1 * t1, 256, -1))
    twist = np.stack(phase(k1 * s, 32768, -1)).astype(np.float32)
    trail = as_real(*phase(k2 * s, 128, -1)).T
    back_trail = as_real(*phase(k2 * s, 128, 1)).T
    back_lead = as_real(*phase(np.arange(128)[:, None] * np.arange(256)[None, :], 256, 1))
    order = [2 * c + t + 128 * part for c in range(64) for part in (0, 1) for t in (0, 1)]
    back_lead = back_lead[np.array(order)]
    return halves(lead), twist, halves(trail), halves(back_trail), halves(back_lead)


def final_tables(total):
    grid = np.arange(64)
    cos, sin = phase(grid[:, None] * grid[None, :], 64, 1)
    full = as_real(cos, sin)
    order = [4 * sub + q + 64 * part for q in range(4) for part in (0, 1) for sub in range(16)]
    rows = full[np.array(order)]
    scale = 0.5 / (math.sqrt(total) * 256.0 * 32768.0)
    mix = np.zeros((4, 64, 4, 2, 16))
    for q in range(4):
        for c in range(64):
            a = 4 * c + q
            for r in range(4):
                cc, ss = phase(a * (4 * r + 1), 1024, 1)
                mix[q, c, r, 0, c % 16] = cc * scale
                mix[q, c, r, 1, c % 16] = -ss * scale
    return halves(rows), halves(mix.reshape(4, 64, 128))


def split(value):
    high = value.astype(BF16)
    return high, (value - high.astype(F32)).astype(BF16)


def dot3(first, second):
    dot = functools.partial(jnp.dot, preferred_element_type=F32)
    return dot(first[0], second[0]) + (dot(first[0], second[1]) + dot(first[1], second[0]))


def place():
    comp, rank = lax.axis_index("comp"), lax.axis_index("rank")
    return {"z": comp // 8, "y": comp % 4, "x": rank // 2 * 2 + comp // 4 % 2, "core": rank % 2}


def device(at):
    return {"comp": (at["z"] * 2 + at["x"] % 2) * 4 + at["y"], "rank": at["x"] // 2 * 2 + at["core"]}


def front_kernel(
    d_ref, row_left_ref, row_right_ref, turn_ref, left_ref, right_ref, out_ref,
    lines_ref, dense_ref, weight_ref, field_ref, one_sem, send_sem, recv_sem,
):
    me = place()
    z, y, x, core = me["z"], me["y"], me["x"], me["core"]
    mine = (z * 2 + x % 2, y)

    def at(**changes):
        moved = dict(me)
        for axis, value in changes.items():
            moved[axis] = value % SIZE[axis] if axis in SIZE else value
        return moved

    def group_x(where):
        return where["x"] % 2 * 4 + where["x"] // 2 * 2 + where["core"]

    def group_y(where):
        return where["y"] * 2 + where["core"]

    loads = [
        pltpu.make_async_copy(d_ref.at[:, row], lines_ref.at[row], one_sem.at[0])
        for row in range(4)
    ]
    for load in loads:
        load.start()
    barrier = pltpu.get_barrier_semaphore()
    friends = [at(z=z + o) for o in range(1, 8)]
    friends += [at(z=z + o, x=x + side) for o in range(8) for side in (1, -1)]
    friends += [at(y=y + o) for o in range(1, 4)]
    friends += [at(y=y + o, x=x + side) for o in range(1, 4) for side in (1, -1)]
    friends += [at(x=x + 2)]
    friends += [at(x=x + o, core=1 - core) for o in range(4)]
    friends += [at(y=y + o, core=1 - core) for o in range(1, 4)]
    for friend in friends:
        pl.semaphore_signal(barrier, inc=1, device_id=device(friend), device_id_type=MESH)

    both = jnp.concatenate([row_left_ref[...], row_right_ref[...]], axis=0)
    for region in (0, 1):
        for p in range(8):
            if region == 0:
                owner = at(x=p // 4 + p % 4 // 2 * 2, core=p % 2)
            else:
                owner = at(y=p // 2, core=p % 2)
            owner = device(owner)
            turn = turn_ref[4 * owner["comp"] + owner["rank"]]
            for part in (0, 1):
                high, low = split(both * turn[part : part + 1])
                first = 32 * p + 16 * part
                weight_ref[region, 0, first : first + 16] = high
                weight_ref[region, 1, first : first + 16] = low

    pltpu.make_async_copy(lines_ref, lines_ref, one_sem.at[0]).wait()
    pl.semaphore_wait(barrier, len(friends))

    def slices(region, where):
        index = group_x(where) if region == 0 else 8 + group_y(where)
        return lines_ref.at[:, pl.ds(pl.multiple_of(8 * index, 8), 8)]

    def spread(region, targets):
        pltpu.make_async_copy(
            slices(region, me), dense_ref.at[(region,) + mine], one_sem.at[3 + region]
        ).start()
        for target in targets:
            pltpu.make_async_remote_copy(
                src_ref=slices(region, target),
                dst_ref=dense_ref.at[(region,) + mine],
                send_sem=one_sem.at[1 + region],
                recv_sem=one_sem.at[3 + region],
                device_id=device(target),
                device_id_type=MESH,
            ).start()

    spread(
        1,
        [at(y=y + o) for o in range(1, 4)]
        + [at(y=y + o, x=x - 1 + (y + o) % 4 % 2 * 2) for o in range(4)],
    )
    spread(
        0,
        [at(z=z + o) for o in range(1, 8)]
        + [at(z=z + o, x=x - 1 + (z + o) % 8 % 2 * 2) for o in range(8)],
    )
    started = []

    def send(block, target):
        i = len(started)
        copy = pltpu.make_async_remote_copy(
            src_ref=block,
            dst_ref=block,
            send_sem=send_sem.at[i],
            recv_sem=recv_sem.at[i],
            device_id=device(target),
            device_id_type=MESH,
        )
        copy.start()
        started.append(copy)
        return copy

    def ring(axis, steps, block):
        ahead = {1: [None, None], -1: [None, None]}
        for step in range(1, steps + 1):
            for turn in (0, 1):
                for way in (1, -1):
                    chunk = turn if way == 1 else 1 - turn
                    if ahead[way][chunk] is not None:
                        ahead[way][chunk].wait_recv()
                        ahead[way][chunk] = None
                    if step < steps or turn == 0:
                        ahead[way][chunk] = send(
                            block((me[axis] - way * (step - 1)) % SIZE[axis], chunk),
                            at(**{axis: me[axis] + way}),
                        )
            yield
        for way in (1, -1):
            for copy in ahead[way]:
                if copy is not None:
                    copy.wait_recv()

    def block_y(index, chunk):
        return dense_ref.at[0, pl.ds(8 * chunk, 8), index]

    def block_z(index, chunk):
        return dense_ref.at[1, 2 * index + chunk]

    whole_z = dense_ref.at[1, pl.ds(2 * z, 2)]
    pltpu.make_async_copy(whole_z, whole_z, one_sem.at[4]).wait()
    ring_z = ring("z", 4, block_z)
    next(ring_z)
    whole_y = dense_ref.at[0, :, y]
    pltpu.make_async_copy(whole_y, whole_y, one_sem.at[3]).wait()
    ring_y = ring("y", 2, block_y)
    next(ring_y)
    next(ring_z)
    next(ring_y)
    next(ring_z)
    next(ring_z)

    def region_fields(region):
        weights = (weight_ref[region, 0], weight_ref[region, 1])
        source = dense_ref.at[region].reshape(256 * 8, 128)
        target = field_ref.at[region].reshape(256 * 8, 128)
        index = group_x(me) if region == 0 else 8 + group_y(me)
        columns = pl.ds(pl.multiple_of(1024 * index, 1024), 1024)
        cols = jnp.concatenate([left_ref[:, columns], right_ref[:, columns]], axis=0)
        for t in range(0, 8, 2):
            pair = jnp.concatenate(
                [source[pl.ds(u, 256, stride=8), :] for u in (t, t + 1)], axis=1
            )
            field = dot3(weights, split(pair))
            field = field.reshape(16, 16, 256) * cols[None, :, t * 128 : t * 128 + 256]
            field = field.reshape(256, 256)
            for u in (0, 1):
                target[pl.ds(t + u, 256, stride=8), :] = field[:, u * 128 : u * 128 + 128]
        own = group_x(me) if region == 0 else group_y(me)
        landing = out_ref.at[:, pl.ds(pl.multiple_of(8 * index, 8), 8)]
        pltpu.make_async_copy(
            field_ref.at[region, pl.ds(32 * own, 32)], landing, one_sem.at[6]
        ).start()
        others = [(o, c) for o in range(4) for c in (0, 1) if (o, c) != (0, 0)]
        for o, c in others:
            if region == 0:
                target_at = at(x=x + o, core=(core + c) % 2)
                p = group_x(target_at)
            else:
                target_at = at(y=y + o, core=(core + c) % 2)
                p = group_y(target_at)
            pltpu.make_async_remote_copy(
                src_ref=field_ref.at[region, pl.ds(32 * p, 32)],
                dst_ref=landing,
                send_sem=one_sem.at[5],
                recv_sem=one_sem.at[6],
                device_id=device(target_at),
                device_id_type=MESH,
            ).start()

    for _ in ring_y:
        pass
    region_fields(0)
    for _ in ring_z:
        pass
    region_fields(1)
    pltpu.make_async_copy(out_ref, out_ref, one_sem.at[6]).wait()
    for copy in started:
        copy.wait_send()
    for region, count in ((0, 15), (1, 7)):
        sent = dense_ref.at[region, pl.ds(0, count), 0]
        pltpu.make_async_copy(sent, sent, one_sem.at[1 + region]).wait()
    sent = field_ref.at[:, pl.ds(0, 224)]
    pltpu.make_async_copy(sent, sent, one_sem.at[5]).wait()


def front(density, row_left, row_right, col_left, col_right):
    a, k = np.arange(256)[None, :], np.arange(256)[:, None]
    turn = np.stack(phase(a * (4 * k + 1), 1024, -1), axis=1).astype(np.float32)
    vmem = pl.BlockSpec(memory_space=pltpu.VMEM)
    return pl.pallas_call(
        front_kernel,
        out_shape=jax.ShapeDtypeStruct((32, 128, 128), F32),
        in_specs=[pl.BlockSpec(memory_space=pl.ANY)] + [vmem] * 5,
        out_specs=pl.BlockSpec(memory_space=pl.ANY),
        scratch_shapes=[
            pltpu.VMEM((4, 128, 128), F32),
            pltpu.VMEM((2, 16, 4, 4, 8, 128), F32),
            pltpu.VMEM((2, 2, 256, 256), BF16),
            pltpu.VMEM((2, 256, 8, 128), F32),
            pltpu.SemaphoreType.DMA((7,)),
            pltpu.SemaphoreType.DMA((24,)),
            pltpu.SemaphoreType.DMA((24,)),
        ],
        compiler_params=pltpu.CompilerParams(
            collective_id=0, has_side_effects=True, vmem_limit_bytes=40 << 20
        ),
    )(density, row_left, row_right, jnp.asarray(turn), col_left, col_right)


def columns_kernel(in_ref, lead_ref, twist_ref, trail_ref, back_trail_ref, back_lead_ref, out_ref, sum_ref):
    step = pl.program_id(0)

    def table(ref):
        return ref[0], ref[1]

    x = jnp.concatenate(
        [jnp.concatenate([in_ref[part, side, 0] for side in (0, 1)], axis=1) for part in (0, 1)], axis=0
    )
    y = dot3(table(lead_ref), split(x))
    spectra = []
    for side in (0, 1):
        real, imag = y[:256, side * 128 : side * 128 + 128], y[256:, side * 128 : side * 128 + 128]
        cos, sin = twist_ref[0], twist_ref[1]
        turned = jnp.concatenate([real * cos - imag * sin, real * sin + imag * cos], axis=1)
        spectra.append(dot3(split(turned), table(trail_ref)))
    left, right = spectra
    lr, li, rr, ri = left[:, :128], left[:, 128:], right[:, :128], right[:, 128:]
    product = jnp.concatenate([lr * rr - li * ri, lr * ri + li * rr], axis=1)

    @pl.when(step == 0)
    def _():
        sum_ref[...] = product

    @pl.when(step > 0)
    def _():
        sum_ref[...] += product

    @pl.when(step == pl.num_programs(0) - 1)
    def _():
        back = dot3(split(sum_ref[...]), table(back_trail_ref))
        real, imag = back[:, :128], back[:, 128:]
        cos, sin = twist_ref[0], twist_ref[1]
        turned = jnp.concatenate([real * cos + imag * sin, imag * cos - real * sin], axis=0)
        out_ref[...] = dot3(table(back_lead_ref), split(turned))


def columns(fields):
    lead, twist, trail, back_trail, back_lead = tables()

    def whole(array):
        return pl.BlockSpec(array.shape, lambda r: (0,) * array.ndim)

    constants = (lead, twist, trail, back_trail, back_lead)
    return pl.pallas_call(
        columns_kernel,
        out_shape=jax.ShapeDtypeStruct((256, 128), F32),
        grid=(8,),
        in_specs=[pl.BlockSpec((2, 2, 1, 128, 128), lambda r: (0, 0, r, 0, 0))]
        + [whole(c) for c in constants],
        out_specs=pl.BlockSpec((256, 128), lambda r: (0, 0)),
        scratch_shapes=[pltpu.VMEM((256, 256), F32)],
        compiler_params=pltpu.CompilerParams(vmem_limit_bytes=40 << 20),
    )(fields.reshape(2, 2, 8, 128, 128), *(jnp.asarray(c) for c in constants))


def finish_kernel(q_ref, rows_ref, mix_ref, out_ref, got_ref, part_ref, all_ref, line_ref, sems):
    comp, rank = lax.axis_index("comp"), lax.axis_index("rank")

    def peer(offset):
        return {"comp": (comp + offset) % 64, "rank": rank}

    def other(offset):
        return {"comp": comp, "rank": (rank + offset) % 4}

    barrier = pltpu.get_barrier_semaphore()

    def greet(i, carry):
        pl.semaphore_signal(barrier, inc=1, device_id=peer(i), device_id_type=MESH)
        return carry

    lax.fori_loop(1, 64, greet, 0)
    for i in range(1, 4):
        pl.semaphore_signal(barrier, inc=1, device_id=other(i), device_id_type=MESH)
    pl.semaphore_wait(barrier, 66)

    def exchange(source, target, send_sem, recv_sem):
        own = pltpu.make_async_copy(source.at[comp], target.at[comp], recv_sem)
        own.start()

        def send(i, carry):
            to = peer(i)
            pltpu.make_async_remote_copy(
                src_ref=source.at[to["comp"]],
                dst_ref=target.at[comp],
                send_sem=send_sem,
                recv_sem=recv_sem,
                device_id=to,
                device_id_type=MESH,
            ).start()
            return carry

        lax.fori_loop(1, 64, send, 0)
        pltpu.make_async_copy(source, target, recv_sem).wait()
        rest = pl.ds(0, 63)
        pltpu.make_async_copy(source.at[rest], target.at[rest], send_sem).wait()

    exchange(q_ref, got_ref, sems.at[0], sems.at[1])
    x = jnp.concatenate(
        [
            jnp.concatenate([got_ref[:, 2 * part + t, :] for t in (0, 1)], axis=1)
            for part in (0, 1)
        ],
        axis=0,
    )
    part = dot3((rows_ref[0], rows_ref[1]), split(x))
    for q in range(4):
        part_ref[q] = part[32 * q : 32 * q + 32]
    own = pltpu.make_async_copy(part_ref.at[rank], all_ref.at[rank], sems.at[2])
    own.start()
    copies = []
    for i in range(1, 4):
        to = other(i)
        copy = pltpu.make_async_remote_copy(
            src_ref=part_ref.at[to["rank"]],
            dst_ref=all_ref.at[rank],
            send_sem=sems.at[3 + i],
            recv_sem=sems.at[6 + i],
            device_id=to,
            device_id_type=MESH,
        )
        copy.start()
        copies.append(copy)
    own.wait()
    for copy in copies:
        copy.wait()
    lines = dot3((mix_ref[0, rank], mix_ref[1, rank]), split(all_ref[...].reshape(128, 256)))
    for t in (0, 1):
        line_ref[:, t, :] = lines[:, t * 128 : t * 128 + 128]
    exchange(line_ref, out_ref, sems.at[3], sems.at[10])


def finish(q, total):
    rows_table, mix = final_tables(total)
    vmem = pl.BlockSpec(memory_space=pltpu.VMEM)
    return pl.pallas_call(
        finish_kernel,
        out_shape=jax.ShapeDtypeStruct((64, 2, 128), F32),
        in_specs=[vmem] * 3,
        out_specs=vmem,
        scratch_shapes=[
            pltpu.VMEM((64, 4, 128), F32),
            pltpu.VMEM((4, 32, 256), F32),
            pltpu.VMEM((4, 32, 256), F32),
            pltpu.VMEM((64, 2, 128), F32),
            pltpu.SemaphoreType.DMA((11,)),
        ],
        compiler_params=pltpu.CompilerParams(
            collective_id=1, has_side_effects=True, vmem_limit_bytes=40 << 20
        ),
    )(q.reshape(64, 4, 128), jnp.asarray(rows_table), jnp.asarray(mix))


def body(density, row_left, col_left, row_right, col_right):
    lines = density.reshape(4, 128, 128).transpose(1, 0, 2)
    fields = front(lines, row_left, row_right, col_left, col_right)
    return finish(columns(fields), 256 * 16384).reshape(1, 16384)


def solution(mesh):
    return jax.shard_map(
        body,
        mesh=mesh,
        in_specs=(P("comp", None), P(), P(), P(), P()),
        out_specs=P(("comp", "rank"), None),
        check_vma=False,
    )
```

time: 132 us -> 85.7 us (0.65)
  Pallas kernels: 113 us -> 79.1 us
  starting transfers between devices: 10.6 us -> 0 us
  waiting for transfers between devices: 2.29 us -> 0 us
  local copies, waits for them, and re-layouts: 4.32 us -> 6.13 us
  other arithmetic: 1.76 us -> 0 us
    pallas_call x2 -> x1, Pallas kernels: 79.1 us -> 45.1 us  [front(): pl.pallas_call(front_kernel, out_shape=jax.ShapeDtypeStruct((32, 128, 128...]
    ppermute x1 -> x0, starting transfers between devices: 10.6 us -> none  [body(): got = lax.ppermute(other, 'rank', [(0, 1), (1, 0), (2, 3), (3, 2)])]
    ppermute x1 -> x0, waiting for transfers between devices: 2.29 us -> none  [body(): got = lax.ppermute(other, 'rank', [(0, 1), (1, 0), (2, 3), (3, 2)])]
    unnamed x21 -> x27, local copies, waits for them, and re-layouts: 4.09 us -> 6.13 us
  transfers between devices with their start and end apart: 1 -> 0, of which waited for: 1 -> 0; matrix products, arithmetic and copies ran while one was open for 0% -> 0% of each run, Pallas kernels for 0% -> 0%
where the time goes in v2:
time: 85.7 us; the launch traced here: 85.4 us
  Pallas kernels  79.1 us (92%)
  local copies, waits for them, and re-layouts  6.13 us (7%)
    pallas_call x1, Pallas kernels, front(): pl.pallas_call(front_kernel, out_shape=jax.ShapeDtypeStruct((32, 128, 128...  45.1 us
    pallas_call x1, Pallas kernels, finish(): pl.pallas_call(finish_kernel, out_shape=jax.ShapeDtypeStruct((64, 2, 128)...  24.5 us
    pallas_call x1, Pallas kernels, columns(): pl.pallas_call(columns_kernel, out_shape=jax.ShapeDtypeStruct((256, 128),...  9.47 us
    unnamed x27, local copies, waits for them, and re-layouts  6.13 us

profile of v2, /device:TPU:1, one launch (start us, length us, event | category | flops | bytes accessed | tf_op | source)
XLA Modules:
  0.0 85.4 jit_solution(8346356823635317606)
XLA Ops:
  0.0 0.0 copy-start
  0.0 1.0 %copy-done = f32[8,16384]{1,0:T(8,128)S(1)} copy-done((f32[8,16384]{1,0:T(8,128)S(1)}, f32[8,16384]{1,0:T(8,128)}, u32[]{:S(2)}) %copy-start) | copy-done | bytes 524312
  1.0 0.0 copy-start.1
  1.0 1.0 %copy-done.1 = f32[8,16384]{1,0:T(8,128)S(1)} copy-done((f32[8,16384]{1,0:T(8,128)S(1)}, f32[8,16384]{1,0:T(8,128)}, u32[]{:S(2)}) %copy-start.1) | copy-done | bytes 524312
  2.1 0.0 copy-start.2
  2.1 1.0 %copy-done.2 = f32[256,2,256]{2,1,0:T(2,128)S(1)} copy-done((f32[256,2,256]{2,1,0:T(2,128)S(1)}, f32[256,2,256]{2,1,0:T(2,128)}, u32[]{:S(2)}) %copy-start.2) | copy-done | bytes 524312
  3.1 0.0 copy-start.8
  3.1 0.9 %copy-done.8 = f32[4,16384]{1,0:T(4,128)S(1)} copy-done((f32[4,16384]{1,0:T(4,128)S(1)}, f32[4,16384]{1,0:T(4,128)}, u32[]{:S(2)}) %copy-start.8) | copy-done | bytes 262168
  4.1 0.0 copy-start.11
  4.1 0.7 copy-done.11
  4.8 0.0 copy-start.12
  4.8 0.7 copy-done.12
  5.5 0.0 copy-start.3
  5.5 0.0 copy-start.4
  5.5 0.0 copy-start.5
  5.5 0.0 copy-start.6
  5.5 0.0 copy-start.7
  5.5 45.1 %shard_map.127 = f32[32,128,128]{2,1,0:T(8,128)S(1)} custom-call(f32[128,4,128]{2,1,0:T(4,128)S(1)} %bitcast.9, f32[8,256]{1,0:T(8,128)S(1)} %copy-done.11, f32[8,256]{1,0:T(8,128)S(1)} %copy-done.12, f32[256,2,256]{2,1,0:T(2,128)S(1)} %copy-done.2, f32[8,16384]{1,0:T(8,128)S(1)} %copy-done, f32[8,16384]{1,0:T(8,128)S(1)} %copy-done.1), custom_call_target="tpu_custom_call" | custom-call | tf_op jit(solution)/shard_map/pallas_call | solution.py:281
  50.6 0.0 copy-start.9
  50.7 0.0 copy-start.10
  50.7 0.0 copy-done.3
  50.7 0.0 copy-done.4
  50.7 0.0 copy-done.5
  50.7 0.0 copy-done.6
  50.7 0.0 copy-done.7
  50.7 9.5 %shard_map.128 = f32[256,128]{1,0:T(8,128)S(1)} custom-call(f32[2,2,8,128,128]{4,3,2,1,0:T(8,128)S(1)} %bitcast.6, bf16[2,512,256]{2,1,0:T(8,128)(2,1)S(1)} %copy-done.4, f32[2,256,128]{2,1,0:T(8,128)S(1)} %copy-done.7, bf16[2,256,256]{2,1,0:T(8,128)(2,1)S(1)} %copy-done.6, bf16[2,256,256]{2,1,0:T(8,128)(2,1)S(1)} %copy-done.5, ...), custom_call_target="tpu_custom_call" | custom-call | tf_op jit(solution)/shard_map/pallas_call | solution.py:345
  60.2 0.0 copy-done.9
  60.2 0.0 copy-done.10
  60.2 24.5 %shard_map.129 = f32[64,2,128]{2,1,0:T(2,128)S(1)} custom-call(f32[64,4,128]{2,1,0:T(4,128)S(1)} %bitcast.7, bf16[2,128,128]{2,1,0:T(8,128)(2,1)S(1)} %copy-done.10, bf16[2,4,64,128]{3,2,1,0:T(8,128)(2,1)S(1)} %copy-done.9), custom_call_target="tpu_custom_call" | custom-call | tf_op jit(solution)/shard_map/pallas_call | solution.py:436
  84.8 0.6 copy.15
Async XLA Ops:
  0.0 1.0 %copy-start = (f32[8,16384]{1,0:T(8,128)S(1)}, f32[8,16384]{1,0:T(8,128)}, u32[]{:S(2)}) copy-start(f32[8,16384]{1,0:T(8,128)} %left_ref.1) | copy-start | bytes 1572868
  1.0 1.0 %copy-start.1 = (f32[8,16384]{1,0:T(8,128)S(1)}, f32[8,16384]{1,0:T(8,128)}, u32[]{:S(2)}) copy-start(f32[8,16384]{1,0:T(8,128)} %right_ref.1) | copy-start | bytes 1572868
  2.1 1.0 %copy-start.2 = (f32[256,2,256]{2,1,0:T(2,128)S(1)}, f32[256,2,256]{2,1,0:T(2,128)}, u32[]{:S(2)}) copy-start(f32[256,2,256]{2,1,0:T(2,128)} %constant.16.clone.turn_ref) | copy-start | bytes 1572868
  3.1 0.9 %copy-start.8 = (f32[4,16384]{1,0:T(4,128)S(1)}, f32[4,16384]{1,0:T(4,128)}, u32[]{:S(2)}) copy-start(f32[4,16384]{1,0:T(4,128)} %param.13) | copy-start | bytes 786436
  4.1 0.7 copy-start.11
  4.8 0.7 copy-start.12
  5.5 45.2 %copy-start.3 = (bf16[2,256,512]{2,1,0:T(8,128)(2,1)S(1)}, bf16[2,256,512]{2,1,0:T(8,128)(2,1)}, u32[]{:S(2)}) copy-start(bf16[2,256,512]{2,1,0:T(8,128)(2,1)} %constant.21.clone.back_lead_ref) | copy-start | bytes 1572868
  5.5 45.2 %copy-start.4 = (bf16[2,512,256]{2,1,0:T(8,128)(2,1)S(1)}, bf16[2,512,256]{2,1,0:T(8,128)(2,1)}, u32[]{:S(2)}) copy-start(bf16[2,512,256]{2,1,0:T(8,128)(2,1)} %constant.17.clone.lead_ref) | copy-start | bytes 1572868
  5.5 45.2 %copy-start.5 = (bf16[2,256,256]{2,1,0:T(8,128)(2,1)S(1)}, bf16[2,256,256]{2,1,0:T(8,128)(2,1)}, u32[]{:S(2)}) copy-start(bf16[2,256,256]{2,1,0:T(8,128)(2,1)} %constant.20.clone.back_trail_ref) | copy-start | bytes 786436
  5.5 45.2 %copy-start.6 = (bf16[2,256,256]{2,1,0:T(8,128)(2,1)S(1)}, bf16[2,256,256]{2,1,0:T(8,128)(2,1)}, u32[]{:S(2)}) copy-start(bf16[2,256,256]{2,1,0:T(8,128)(2,1)} %constant.19.clone.trail_ref) | copy-start | bytes 786436
  5.5 45.2 %copy-start.7 = (f32[2,256,128]{2,1,0:T(8,128)S(1)}, f32[2,256,128]{2,1,0:T(8,128)}, u32[]{:S(2)}) copy-start(f32[2,256,128]{2,1,0:T(8,128)} %constant.18.clone.twist_ref) | copy-start | bytes 786436
  50.6 9.6 %copy-start.9 = (bf16[2,4,64,128]{3,2,1,0:T(8,128)(2,1)S(1)}, bf16[2,4,64,128]{3,2,1,0:T(8,128)(2,1)}, u32[]{:S(2)}) copy-start(bf16[2,4,64,128]{3,2,1,0:T(8,128)(2,1)} %constant.23.clone.mix_ref) | copy-start | bytes 393220
  50.7 9.6 %copy-start.10 = (bf16[2,128,128]{2,1,0:T(8,128)(2,1)S(1)}, bf16[2,128,128]{2,1,0:T(8,128)(2,1)}, u32[]{:S(2)}) copy-start(bf16[2,128,128]{2,1,0:T(8,128)(2,1)} %constant.22.clone.rows_ref) | copy-start | bytes 196612

commit v3 on v2

v3 whole, which is shorter than its diff:
```python
import functools
import math

import jax
import jax.numpy as jnp
import ml_dtypes
import numpy as np
from jax import lax
from jax.experimental import pallas as pl
from jax.experimental.pallas import tpu as pltpu
from jax.sharding import PartitionSpec as P

MESH = pl.DeviceIdType.MESH
BF16 = jnp.bfloat16
F32 = jnp.float32
SIZE = {"x": 4, "y": 4, "z": 8}


def halves(table):
    table = np.asarray(table, np.float64)
    high = table.astype(ml_dtypes.bfloat16)
    low = (table - high.astype(np.float64)).astype(ml_dtypes.bfloat16)
    return np.stack([high, low])


def phase(numerator, length, sign):
    angle = sign * 2.0 * np.pi * (np.asarray(numerator) % length) / length
    return np.cos(angle), np.sin(angle)


def as_real(cos, sin):
    return np.block([[cos, -sin], [sin, cos]])


def tables(total):
    k1, t1 = np.arange(256)[:, None], np.arange(128)[None, :]
    k2, s = np.arange(128)[:, None], np.arange(128)[None, :]
    a, k = np.arange(256)[None, :], np.arange(256)[:, None]
    turn = np.stack(phase(a * (4 * k + 1), 1024, -1), axis=1).astype(np.float32)
    lead = as_real(*phase(k1 * t1, 256, -1))
    twist = np.stack(phase(k1 * s, 32768, -1)).astype(np.float32)
    trail = as_real(*phase(k2 * s, 128, -1)).T
    back_trail = as_real(*phase(k2 * s, 128, 1)).T
    back_lead = as_real(*phase(np.arange(128)[:, None] * np.arange(256)[None, :], 256, 1))
    order = [8 * i + t + 128 * part for i in range(16) for part in (0, 1) for t in range(8)]
    back_lead = back_lead[np.array(order)]
    scale = 0.5 / (math.sqrt(total) * 256.0 * 32768.0)
    j, a0 = np.arange(16)[:, None], np.arange(16)[None, :]
    middle = scale * np.stack(phase(a0 * (4 * j + 1), 1024, 1), axis=2).reshape(16, 32, 1)
    middle = np.broadcast_to(middle, (16, 32, 128)).astype(np.float32)
    return turn, halves(lead), twist, halves(trail), halves(back_trail), halves(back_lead), middle


def scaled(value, numerator, length):
    real, imag = value
    cos, sin = (float(v) for v in phase(numerator, length, 1))
    if numerator == 0:
        return value
    if 4 * numerator == length:
        return -imag, real
    return real * cos - imag * sin, real * sin + imag * cos


def short_dft(values):
    length = len(values)
    if length == 1:
        return values
    even, odd = short_dft(values[0::2]), short_dft(values[1::2])
    odd = [scaled(v, n, length) for n, v in enumerate(odd)]
    pairs = list(zip(even, odd))
    return [(e[0] + o[0], e[1] + o[1]) for e, o in pairs] + [
        (e[0] - o[0], e[1] - o[1]) for e, o in pairs
    ]


def split(value):
    high = value.astype(BF16)
    return high, (value - high.astype(F32)).astype(BF16)


def dot3(first, second):
    dot = functools.partial(jnp.dot, preferred_element_type=F32)
    return dot(first[0], second[0]) + (dot(first[0], second[1]) + dot(first[1], second[0]))


def place():
    comp, rank = lax.axis_index("comp"), lax.axis_index("rank")
    return {"z": comp // 8, "y": comp % 4, "x": rank // 2 * 2 + comp // 4 % 2, "core": rank % 2}


def device(at):
    return {"comp": (at["z"] * 2 + at["x"] % 2) * 4 + at["y"], "rank": at["x"] // 2 * 2 + at["core"]}


def kernel(
    d_ref, row_left_ref, row_right_ref, left_ref, right_ref,
    turn_hbm, lead_hbm, twist_hbm, trail_hbm, back_trail_hbm, back_lead_hbm, middle_hbm,
    out_ref,
    lines_ref, dense_ref, weight_ref, field_ref, all_ref, cols_ref,
    turn_ref, lead_ref, twist_ref, trail_ref, back_trail_ref, back_lead_ref, middle_ref,
    sum_ref, conv_ref, got_ref, part_ref, line_ref,
    one_sem, send_sem, recv_sem,
):
    me = place()
    z, y, x, core = me["z"], me["y"], me["x"], me["core"]
    mine = (z * 2 + x % 2, y)

    def at(**changes):
        moved = dict(me)
        for axis, value in changes.items():
            moved[axis] = value % SIZE[axis] if axis in SIZE else value
        return moved

    def group_x(where):
        return where["x"] % 2 * 4 + where["x"] // 2 * 2 + where["core"]

    def group_y(where):
        return where["y"] * 2 + where["core"]

    def group(region, where):
        return group_x(where) if region == 0 else group_y(where)

    def member(region, p):
        if region == 0:
            return at(x=p // 4 + p % 4 // 2 * 2, core=p % 2)
        return at(y=p // 2, core=p % 2)

    for row in range(4):
        pltpu.make_async_copy(d_ref.at[:, row], lines_ref.at[row], one_sem.at[0]).start()
    barrier = pltpu.get_barrier_semaphore()
    friends = [at(z=z + o) for o in range(1, 8)]
    friends += [at(z=z + o, x=x + side) for o in range(8) for side in (1, -1)]
    friends += [at(y=y + o) for o in range(1, 4)]
    friends += [at(y=y + o, x=x + side) for o in range(1, 4) for side in (1, -1)]
    friends += [at(x=x + 2)]
    friends += [at(x=x + o, core=1 - core) for o in range(4)]
    friends += [at(y=y + o, core=1 - core) for o in range(1, 4)]
    friends += [at(y=y + o, x=x + 2, core=c) for o in range(1, 4) for c in (0, 1)]
    for friend in friends:
        pl.semaphore_signal(barrier, inc=1, device_id=device(friend), device_id_type=MESH)

    for region in (0, 1):
        for p in range(8):
            owner = device(member(region, p))
            pltpu.make_async_copy(
                turn_hbm.at[4 * owner["comp"] + owner["rank"]],
                turn_ref.at[8 * region + p],
                one_sem.at[7],
            ).start()
    for region in (0, 1):
        columns = pl.ds(pl.multiple_of(1024 * (8 * region + group(region, me)), 1024), 1024)
        for side, source in enumerate((left_ref, right_ref)):
            pltpu.make_async_copy(
                source.at[:, columns], cols_ref.at[region, pl.ds(8 * side, 8)], one_sem.at[8]
            ).start()
    mine_j = y * 4 + x // 2 * 2 + core
    mine_i = z * 2 + x % 2
    for source, target in (
        (lead_hbm, lead_ref),
        (twist_hbm, twist_ref),
        (trail_hbm, trail_ref),
        (back_trail_hbm, back_trail_ref),
        (back_lead_hbm, back_lead_ref),
        (middle_hbm.at[mine_j], middle_ref),
    ):
        pltpu.make_async_copy(source, target, one_sem.at[9]).start()
    pltpu.make_async_copy(turn_ref, turn_ref, one_sem.at[7]).wait()
    both = jnp.concatenate([row_left_ref[...], row_right_ref[...]], axis=0)
    for region in (0, 1):
        for p in range(8):
            turn = turn_ref[8 * region + p]
            for part in (0, 1):
                high, low = split(both * turn[part : part + 1])
                first = 32 * p + 16 * part
                weight_ref[region, 0, first : first + 16] = high
                weight_ref[region, 1, first : first + 16] = low

    pltpu.make_async_copy(lines_ref, lines_ref, one_sem.at[0]).wait()
    pl.semaphore_wait(barrier, len(friends))

    def slices(region, where):
        index = group_x(where) if region == 0 else 8 + group_y(where)
        return lines_ref.at[:, pl.ds(pl.multiple_of(8 * index, 8), 8)]

    def spread(region, targets):
        pltpu.make_async_copy(
            slices(region, me), dense_ref.at[(region,) + mine], one_sem.at[3 + region]
        ).start()
        for target in targets:
            pltpu.make_async_remote_copy(
                src_ref=slices(region, target),
                dst_ref=dense_ref.at[(region,) + mine],
                send_sem=one_sem.at[1 + region],
                recv_sem=one_sem.at[3 + region],
                device_id=device(target),
                device_id_type=MESH,
            ).start()

    spread(
        1,
        [at(y=y + o) for o in range(1, 4)]
        + [at(y=y + o, x=x - 1 + (y + o) % 4 % 2 * 2) for o in range(4)],
    )
    spread(
        0,
        [at(z=z + o) for o in range(1, 8)]
        + [at(z=z + o, x=x - 1 + (z + o) % 8 % 2 * 2) for o in range(8)],
    )
    started = []

    def send(block, target):
        i = len(started)
        copy = pltpu.make_async_remote_copy(
            src_ref=block,
            dst_ref=block,
            send_sem=send_sem.at[i],
            recv_sem=recv_sem.at[i],
            device_id=device(target),
            device_id_type=MESH,
        )
        copy.start()
        started.append(copy)
        return copy

    def ring(axis, steps, block):
        ahead = {1: [None, None], -1: [None, None]}
        for step in range(1, steps + 1):
            for turn in (0, 1):
                for way in (1, -1):
                    chunk = turn if way == 1 else 1 - turn
                    if ahead[way][chunk] is not None:
                        ahead[way][chunk].wait_recv()
                        ahead[way][chunk] = None
                    if step < steps or turn == 0:
                        ahead[way][chunk] = send(
                            block((me[axis] - way * (step - 1)) % SIZE[axis], chunk),
                            at(**{axis: me[axis] + way}),
                        )
            yield
        for way in (1, -1):
            for copy in ahead[way]:
                if copy is not None:
                    copy.wait_recv()

    def block_y(index, chunk):
        return dense_ref.at[0, pl.ds(8 * chunk, 8), index]

    def block_z(index, chunk):
        return dense_ref.at[1, 2 * index + chunk]

    whole_z = dense_ref.at[1, pl.ds(2 * z, 2)]
    pltpu.make_async_copy(whole_z, whole_z, one_sem.at[4]).wait()
    ring_z = ring("z", 4, block_z)
    next(ring_z)
    whole_y = dense_ref.at[0, :, y]
    pltpu.make_async_copy(whole_y, whole_y, one_sem.at[3]).wait()
    ring_y = ring("y", 2, block_y)
    next(ring_y)
    next(ring_z)
    next(ring_y)
    next(ring_z)
    next(ring_z)

    counts = (1, 4)

    def region_fields(region):
        weights = (weight_ref[region, 0], weight_ref[region, 1])
        source = dense_ref.at[region].reshape(256 * 8, 128)
        target = field_ref.at[region].reshape(256 * 8, 128)
        for t in range(0, 8, 2):
            pair = jnp.concatenate(
                [source[pl.ds(u, 256, stride=8), :] for u in (t, t + 1)], axis=1
            )
            field = dot3(weights, split(pair))
            cols = cols_ref[region, :, t * 128 : t * 128 + 256]
            field = (field.reshape(16, 16, 256) * cols[None]).reshape(256, 256)
            for u in (0, 1):
                target[pl.ds(t + u, 256, stride=8), :] = field[:, u * 128 : u * 128 + 128]
        own = group(region, me)
        place_t = pl.ds(pl.multiple_of(64 * region + 8 * own, 8), 8)
        terms = 8 // counts[region]
        for chunk in range(counts[region]):
            which = pl.ds(terms * chunk, terms)
            landing = all_ref.at[:, which, place_t]
            recv = one_sem.at[10 + 4 * region + chunk]
            pltpu.make_async_copy(field_ref.at[region, own, :, which], landing, recv).start()
            for o, c in [(2, 0), (2, 1), (1, 0), (3, 1), (1, 1), (3, 0), (0, 1)]:
                moved = {"core": (core + c) % 2, "xy"[region]: me["xy"[region]] + o}
                moved = at(**moved)
                pltpu.make_async_remote_copy(
                    src_ref=field_ref.at[region, group(region, moved), :, which],
                    dst_ref=landing,
                    send_sem=one_sem.at[5],
                    recv_sem=recv,
                    device_id=device(moved),
                    device_id_type=MESH,
                ).start()

    def arrived(region, chunk):
        terms = 8 // counts[region]
        block = all_ref.at[:, pl.ds(terms * chunk, terms), pl.ds(64 * region, 64)]
        pltpu.make_async_copy(block, block, one_sem.at[10 + 4 * region + chunk]).wait()

    def table(ref):
        return ref[0], ref[1]

    def convolve(r, carry):
        x = jnp.concatenate(
            [
                jnp.concatenate([all_ref[2 * part + side, r] for side in (0, 1)], axis=1)
                for part in (0, 1)
            ],
            axis=0,
        )
        y = dot3(table(lead_ref), split(x))
        spectra = []
        for side in (0, 1):
            lanes = slice(side * 128, side * 128 + 128)
            real, imag = y[:256, lanes], y[256:, lanes]
            cos, sin = twist_ref[0], twist_ref[1]
            turned = jnp.concatenate([real * cos - imag * sin, real * sin + imag * cos], axis=1)
            spectra.append(dot3(split(turned), table(trail_ref)))
        left, right = spectra
        lr, li, rr, ri = left[:, :128], left[:, 128:], right[:, :128], right[:, 128:]
        sum_ref[:, :128] += lr * rr - li * ri
        sum_ref[:, 128:] += lr * ri + li * rr
        return carry

    pltpu.make_async_copy(cols_ref, cols_ref, one_sem.at[8]).wait()
    for _ in ring_y:
        pass
    region_fields(0)
    for _ in ring_z:
        pass
    region_fields(1)
    sum_ref[...] = jnp.zeros_like(sum_ref)
    for target in (lead_ref, twist_ref, trail_ref, back_trail_ref, back_lead_ref, middle_ref):
        pltpu.make_async_copy(target, target, one_sem.at[9]).wait()
    arrived(0, 0)
    for chunk in range(4):
        arrived(1, chunk)
        lax.fori_loop(2 * chunk, 2 * chunk + 2, convolve, 0)

    back = dot3(split(sum_ref[...]), table(back_trail_ref))
    real, imag = back[:, :128], back[:, 128:]
    cos, sin = twist_ref[0], twist_ref[1]
    turned = jnp.concatenate([real * cos + imag * sin, imag * cos - real * sin], axis=0)
    conv_ref[...] = dot3(table(back_lead_ref), split(turned)).reshape(16, 16, 128)

    def by_i(i):
        return at(z=i // 2, x=x // 2 * 2 + i % 2)

    def by_j(j):
        return at(y=j // 4, x=j % 4 // 2 * 2 + x % 2, core=j % 2)

    def exchange(source, target, to, own, sems):
        pltpu.make_async_copy(source.at[own], target.at[own], sems[1]).start()
        for o in range(1, 16):
            index = (own + o) % 16
            pltpu.make_async_remote_copy(
                src_ref=source.at[index],
                dst_ref=target.at[own],
                send_sem=sems[0],
                recv_sem=sems[1],
                device_id=device(to(index)),
                device_id_type=MESH,
            ).start()
        pltpu.make_async_copy(target, target, sems[1]).wait()

    exchange(conv_ref, got_ref.at[0], by_i, mine_i, (one_sem.at[18], one_sem.at[19]))
    values = [(got_ref[0, i, :8], got_ref[0, i, 8:]) for i in range(16)]
    for a, (real, imag) in enumerate(short_dft(values)):
        cos, sin = middle_ref[2 * a : 2 * a + 1], middle_ref[2 * a + 1 : 2 * a + 2]
        part_ref[a, :8] = real * cos - imag * sin
        part_ref[a, 8:] = real * sin + imag * cos
    exchange(part_ref, got_ref.at[1], by_j, mine_j, (one_sem.at[20], one_sem.at[21]))
    values = [(got_ref[1, i, :8], got_ref[1, i, 8:]) for i in range(16)]
    for a, value in enumerate(short_dft(values)):
        line_ref[a] = scaled(value, a, 64)[0]
    exchange(line_ref, out_ref, by_i, mine_i, (one_sem.at[22], one_sem.at[23]))

    for copy in started:
        copy.wait_send()
    for region, count in ((0, 15), (1, 7)):
        sent = dense_ref.at[region, pl.ds(0, count), 0]
        pltpu.make_async_copy(sent, sent, one_sem.at[1 + region]).wait()
    sent = field_ref.at[:, pl.ds(0, 7)]
    pltpu.make_async_copy(sent, sent, one_sem.at[5]).wait()
    for source, sem in ((conv_ref, 18), (part_ref, 20), (line_ref, 22)):
        sent = source.at[pl.ds(0, 15)]
        pltpu.make_async_copy(sent, sent, one_sem.at[sem]).wait()


def body(density, row_left, col_left, row_right, col_right):
    lines = density.reshape(4, 128, 128).transpose(1, 0, 2)
    constants = [jnp.asarray(c) for c in tables(256 * 16384)]
    vmem = pl.BlockSpec(memory_space=pltpu.VMEM)
    here = pl.BlockSpec(memory_space=pl.ANY)
    out = pl.pallas_call(
        kernel,
        out_shape=jax.ShapeDtypeStruct((16, 8, 128), F32),
        in_specs=[here, vmem, vmem] + [here] * 9,
        out_specs=here,
        scratch_shapes=[
            pltpu.VMEM((4, 128, 128), F32),
            pltpu.VMEM((2, 16, 4, 4, 8, 128), F32),
            pltpu.VMEM((2, 2, 256, 256), BF16),
            pltpu.VMEM((2, 8, 4, 8, 8, 128), F32),
            pltpu.VMEM((4, 8, 128, 128), F32),
            pltpu.VMEM((2, 16, 1024), F32),
            pltpu.VMEM((16, 2, 256), F32),
            pltpu.VMEM((2, 512, 256), BF16),
            pltpu.VMEM((2, 256, 128), F32),
            pltpu.VMEM((2, 256, 256), BF16),
            pltpu.VMEM((2, 256, 256), BF16),
            pltpu.VMEM((2, 256, 512), BF16),
            pltpu.VMEM((32, 128), F32),
            pltpu.VMEM((256, 256), F32),
            pltpu.VMEM((16, 16, 128), F32),
            pltpu.VMEM((2, 16, 16, 128), F32),
            pltpu.VMEM((16, 16, 128), F32),
            pltpu.VMEM((16, 8, 128), F32),
            pltpu.SemaphoreType.DMA((24,)),
            pltpu.SemaphoreType.DMA((24,)),
            pltpu.SemaphoreType.DMA((24,)),
        ],
        compiler_params=pltpu.CompilerParams(
            collective_id=0, has_side_effects=True, vmem_limit_bytes=60 << 20
        ),
    )(lines, row_left, row_right, col_left, col_right, *constants)
    return out.reshape(1, 16384)


def solution(mesh):
    return jax.shard_map(
        body,
        mesh=mesh,
        in_specs=(P("comp", None), P(), P(), P(), P()),
        out_specs=P(("comp", "rank"), None),
        check_vma=False,
    )
```

time: 85.7 us -> 72.1 us (0.84)
  Pallas kernels: 79.1 us -> 70.5 us
  local copies, waits for them, and re-layouts: 6.13 us -> 1.47 us
    pallas_call x3 -> x1, Pallas kernels: 79.1 us -> 70.5 us  [body(): pl.pallas_call(kernel, out_shape=jax.ShapeDtypeStruct((16, 8, 128), F32),...]
    unnamed x27 -> x1, local copies, waits for them, and re-layouts: 6.13 us -> 1.47 us
where the time goes in v3:
time: 72.1 us; the launch traced here: 71.9 us
  Pallas kernels  70.5 us (98%)
  local copies, waits for them, and re-layouts  1.47 us (2%)
    pallas_call x1, Pallas kernels, body(): pl.pallas_call(kernel, out_shape=jax.ShapeDtypeStruct((16, 8, 128), F32),...  70.5 us
    unnamed x1, local copies, waits for them, and re-layouts  1.47 us

profile of v3, /device:TPU:1, one launch (start us, length us, event | category | flops | bytes accessed | tf_op | source)
XLA Modules:
  0.0 71.9 jit_solution(4160574992892726344)
XLA Ops:
  0.0 70.5 %shard_map.118 = f32[16,8,128]{2,1,0:T(8,128)} custom-call(f32[128,4,128]{2,1,0:T(4,128)} %bitcast.5, f32[8,256]{1,0:T(8,128)} %row_left_ref.1, f32[8,256]{1,0:T(8,128)} %row_right_ref.1, f32[8,16384]{1,0:T(8,128)} %left_ref.1, f32[8,16384]{1,0:T(8,128)} %right_ref.1, f32[256,2,256]{2,1,0:T(2,128)} %constant.14.clone.turn_hbm, ...), custom_call_target="tpu_custom_call" | custom-call | tf_op jit(solution)/shard_map/pallas_call | solution.py:399
  70.5 1.5 %copy.14 = f32[1,16384]{1,0:T(1,128)} copy(f32[1,16384]{1,0:T(1,128)} %bitcast.4) | data formatting | bytes 131072

commit v4 on v3

--- a/solution.py
+++ b/solution.py
@@ -14,6 +14,7 @@
 BF16 = jnp.bfloat16
 F32 = jnp.float32
 SIZE = {"x": 4, "y": 4, "z": 8}
+AHEAD = 4
 
 
 def halves(table):
@@ -99,7 +100,7 @@
     lines_ref, dense_ref, weight_ref, field_ref, all_ref, cols_ref,
     turn_ref, lead_ref, twist_ref, trail_ref, back_trail_ref, back_lead_ref, middle_ref,
     sum_ref, conv_ref, got_ref, part_ref, line_ref,
-    one_sem, send_sem, recv_sem,
+    one_sem, send_sem, recv_sem, pair_sem,
 ):
     me = place()
     z, y, x, core = me["z"], me["y"], me["x"], me["core"]
@@ -126,16 +127,12 @@
         return at(y=p // 2, core=p % 2)
 
     for row in range(4):
-        pltpu.make_async_copy(d_ref.at[:, row], lines_ref.at[row], one_sem.at[0]).start()
+        pltpu.make_async_copy(d_ref.at[:, :, row], lines_ref.at[:, row], one_sem.at[0]).start()
     barrier = pltpu.get_barrier_semaphore()
     friends = [at(z=z + o) for o in range(1, 8)]
-    friends += [at(z=z + o, x=x + side) for o in range(8) for side in (1, -1)]
     friends += [at(y=y + o) for o in range(1, 4)]
-    friends += [at(y=y + o, x=x + side) for o in range(1, 4) for side in (1, -1)]
-    friends += [at(x=x + 2)]
-    friends += [at(x=x + o, core=1 - core) for o in range(4)]
-    friends += [at(y=y + o, core=1 - core) for o in range(1, 4)]
-    friends += [at(y=y + o, x=x + 2, core=c) for o in range(1, 4) for c in (0, 1)]
+    friends += [at(x=x + o) for o in range(1, 4)]
+    friends += [at(core=1 - core)]
     for friend in friends:
         pl.semaphore_signal(barrier, inc=1, device_id=device(friend), device_id_type=MESH)
 
@@ -177,35 +174,39 @@
 
     pltpu.make_async_copy(lines_ref, lines_ref, one_sem.at[0]).wait()
     pl.semaphore_wait(barrier, len(friends))
+    pl.semaphore_signal(
+        pair_sem, inc=1, device_id=device(at(core=1 - core)), device_id_type=MESH
+    )
 
     def slices(region, where):
-        index = group_x(where) if region == 0 else 8 + group_y(where)
-        return lines_ref.at[:, pl.ds(pl.multiple_of(8 * index, 8), 8)]
-
-    def spread(region, targets):
-        pltpu.make_async_copy(
-            slices(region, me), dense_ref.at[(region,) + mine], one_sem.at[3 + region]
+        return lines_ref.at[8 * region + group(region, where)]
+
+    def copy(source, block, sender, receiver, target):
+        pltpu.make_async_remote_copy(
+            src_ref=source,
+            dst_ref=block,
+            send_sem=sender,
+            recv_sem=receiver,
+            device_id=device(target),
+            device_id_type=MESH,
         ).start()
-        for target in targets:
-            pltpu.make_async_remote_copy(
-                src_ref=slices(region, target),
-                dst_ref=dense_ref.at[(region,) + mine],
-                send_sem=one_sem.at[1 + region],
-                recv_sem=one_sem.at[3 + region],
-                device_id=device(target),
-                device_id_type=MESH,
-            ).start()
-
-    spread(
-        1,
-        [at(y=y + o) for o in range(1, 4)]
-        + [at(y=y + o, x=x - 1 + (y + o) % 4 % 2 * 2) for o in range(4)],
-    )
-    spread(
-        0,
-        [at(z=z + o) for o in range(1, 8)]
-        + [at(z=z + o, x=x - 1 + (z + o) % 8 % 2 * 2) for o in range(8)],
-    )
+
+    def await_block(block, sem):
+        pltpu.make_async_copy(block, block, sem).wait()
+
+    near = [1, 7, 2, 6, 3, 5, 4]
+    first_block = dense_ref.at[(0,) + mine]
+    second_block = dense_ref.at[(1,) + mine]
+    beside = at(x=x - 1 + z % 2 * 2)
+    copy(slices(0, beside), first_block, one_sem.at[1], one_sem.at[24], beside)
+    for o in range(1, 4):
+        target = at(y=y + o)
+        copy(slices(1, target), second_block, one_sem.at[2], one_sem.at[4], target)
+    for o in near:
+        copy(slices(0, me), first_block, one_sem.at[1], one_sem.at[24 + o], at(z=z + o))
+    own = pltpu.make_async_copy(slices(0, me), first_block, one_sem.at[3])
+    own.start()
+    pltpu.make_async_copy(slices(1, me), second_block, one_sem.at[4]).start()
     started = []
 
     def send(block, target):
@@ -242,24 +243,41 @@
                 if copy is not None:
                     copy.wait_recv()
 
-    def block_y(index, chunk):
-        return dense_ref.at[0, pl.ds(8 * chunk, 8), index]
-
     def block_z(index, chunk):
-        return dense_ref.at[1, 2 * index + chunk]
-
-    whole_z = dense_ref.at[1, pl.ds(2 * z, 2)]
-    pltpu.make_async_copy(whole_z, whole_z, one_sem.at[4]).wait()
+        return dense_ref.at[1, 2 * index + x % 2, pl.ds(2 * chunk, 2)]
+
+    def along_y(o):
+        block = dense_ref.at[0, pl.ds((z - o) % 8 * 2, 2), y]
+        if o:
+            await_block(block, one_sem.at[24 + o])
+        for step in (2, 1, 3):
+            copy(block, block, one_sem.at[32], one_sem.at[33], at(y=y + step))
+
+    def along_x(o):
+        index = (z + o) % 8
+        block = dense_ref.at[1, 2 * index + x % 2]
+        copy(block, block, one_sem.at[34], one_sem.at[35], at(x=x + 1 - index % 2 * 2))
+
+    other_block = dense_ref.at[0, z * 2 + 1 - x % 2, y]
+    await_block(other_block, one_sem.at[24])
+    for o in near:
+        copy(other_block, other_block, one_sem.at[36], one_sem.at[24 + o], at(z=z + o))
+    own.wait()
+    along_y(0)
+    await_block(dense_ref.at[1, z * 2 + x % 2], one_sem.at[4])
     ring_z = ring("z", 4, block_z)
     next(ring_z)
-    whole_y = dense_ref.at[0, :, y]
-    pltpu.make_async_copy(whole_y, whole_y, one_sem.at[3]).wait()
-    ring_y = ring("y", 2, block_y)
-    next(ring_y)
-    next(ring_z)
-    next(ring_y)
-    next(ring_z)
-    next(ring_z)
+    along_x(0)
+    for step in (1, 2, 3):
+        next(ring_z)
+        along_x(step)
+        along_x(-step)
+        along_y(step)
+        along_y(8 - step)
+    along_y(4)
+    for _ in ring_z:
+        pass
+    along_x(4)
 
     counts = (1, 4)
 
@@ -275,39 +293,38 @@
             cols = cols_ref[region, :, t * 128 : t * 128 + 256]
             field = (field.reshape(16, 16, 256) * cols[None]).reshape(256, 256)
             for u in (0, 1):
-                target[pl.ds(t + u, 256, stride=8), :] = field[:, u * 128 : u * 128 + 128]
+                lanes = slice(u * 128, u * 128 + 128)
+                for p in range(8):
+                    for kind in range(4):
+                        low = 32 * p + 8 * kind
+                        at_rows = pl.ds(256 * p + 8 * kind + t + u, 8, stride=32)
+                        target[at_rows, :] = field[low : low + 8, lanes]
+
+    def send_fields(region, chunk):
         own = group(region, me)
-        place_t = pl.ds(pl.multiple_of(64 * region + 8 * own, 8), 8)
         terms = 8 // counts[region]
-        for chunk in range(counts[region]):
-            which = pl.ds(terms * chunk, terms)
-            landing = all_ref.at[:, which, place_t]
-            recv = one_sem.at[10 + 4 * region + chunk]
-            pltpu.make_async_copy(field_ref.at[region, own, :, which], landing, recv).start()
-            for o, c in [(2, 0), (2, 1), (1, 0), (3, 1), (1, 1), (3, 0), (0, 1)]:
-                moved = {"core": (core + c) % 2, "xy"[region]: me["xy"[region]] + o}
-                moved = at(**moved)
-                pltpu.make_async_remote_copy(
-                    src_ref=field_ref.at[region, group(region, moved), :, which],
-                    dst_ref=landing,
-                    send_sem=one_sem.at[5],
-                    recv_sem=recv,
-                    device_id=device(moved),
-                    device_id_type=MESH,
-                ).start()
+        which = pl.ds(terms * chunk, terms)
+        landing = all_ref.at[8 * region + own, which]
+        recv = one_sem.at[10 + 4 * region + chunk]
+        pltpu.make_async_copy(field_ref.at[region, own, which], landing, recv).start()
+        for o, c in [(2, 0), (2, 1), (1, 0), (3, 1), (1, 1), (3, 0), (0, 1)]:
+            moved = {"core": (core + c) % 2, "xy"[region]: me["xy"[region]] + o}
+            moved = at(**moved)
+            source = field_ref.at[region, group(region, moved), which]
+            copy(source, landing, one_sem.at[5], recv, moved)
 
     def arrived(region, chunk):
         terms = 8 // counts[region]
-        block = all_ref.at[:, pl.ds(terms * chunk, terms), pl.ds(64 * region, 64)]
+        block = all_ref.at[pl.ds(8 * region, 8), pl.ds(terms * chunk, terms)]
         pltpu.make_async_copy(block, block, one_sem.at[10 + 4 * region + chunk]).wait()
 
     def table(ref):
         return ref[0], ref[1]
 
-    def convolve(r, carry):
+    def convolve(r):
         x = jnp.concatenate(
             [
-                jnp.concatenate([all_ref[2 * part + side, r] for side in (0, 1)], axis=1)
+                jnp.concatenate([all_ref[:, r, 2 * part + side].reshape(128, 128) for side in (0, 1)], axis=1)
                 for part in (0, 1)
             ],
             axis=0,
@@ -324,22 +341,26 @@
         lr, li, rr, ri = left[:, :128], left[:, 128:], right[:, :128], right[:, 128:]
         sum_ref[:, :128] += lr * rr - li * ri
         sum_ref[:, 128:] += lr * ri + li * rr
-        return carry
 
     pltpu.make_async_copy(cols_ref, cols_ref, one_sem.at[8]).wait()
-    for _ in ring_y:
-        pass
+    await_block(dense_ref.at[0, :, pl.ds(0, 3)], one_sem.at[33])
+    pl.semaphore_wait(pair_sem, 1)
     region_fields(0)
-    for _ in ring_z:
-        pass
+    send_fields(0, 0)
+    await_block(dense_ref.at[1, pl.ds(0, 8)], one_sem.at[35])
     region_fields(1)
+    for chunk in range(AHEAD):
+        send_fields(1, chunk)
     sum_ref[...] = jnp.zeros_like(sum_ref)
     for target in (lead_ref, twist_ref, trail_ref, back_trail_ref, back_lead_ref, middle_ref):
         pltpu.make_async_copy(target, target, one_sem.at[9]).wait()
     arrived(0, 0)
     for chunk in range(4):
         arrived(1, chunk)
-        lax.fori_loop(2 * chunk, 2 * chunk + 2, convolve, 0)
+        if chunk + AHEAD < 4:
+            send_fields(1, chunk + AHEAD)
+        convolve(2 * chunk)
+        convolve(2 * chunk + 1)
 
     back = dot3(split(sum_ref[...]), table(back_trail_ref))
     real, imag = back[:, :128], back[:, 128:]
@@ -381,9 +402,14 @@
 
     for copy in started:
         copy.wait_send()
-    for region, count in ((0, 15), (1, 7)):
-        sent = dense_ref.at[region, pl.ds(0, count), 0]
-        pltpu.make_async_copy(sent, sent, one_sem.at[1 + region]).wait()
+    for sent, sem in (
+        (dense_ref.at[0, pl.ds(0, 8), 0], 1),
+        (dense_ref.at[0, pl.ds(0, 3), 0], 2),
+        (dense_ref.at[0, :, pl.ds(0, 3)], 32),
+        (dense_ref.at[1, pl.ds(0, 8)], 34),
+        (dense_ref.at[0, pl.ds(0, 7), 0], 36),
+    ):
+        await_block(sent, one_sem.at[sem])
     sent = field_ref.at[:, pl.ds(0, 7)]
     pltpu.make_async_copy(sent, sent, one_sem.at[5]).wait()
     for source, sem in ((conv_ref, 18), (part_ref, 20), (line_ref, 22)):
@@ -392,7 +418,7 @@
 
 
 def body(density, row_left, col_left, row_right, col_right):
-    lines = density.reshape(4, 128, 128).transpose(1, 0, 2)
+    lines = density.reshape(4, 16, 8, 128).transpose(1, 2, 0, 3)
     constants = [jnp.asarray(c) for c in tables(256 * 16384)]
     vmem = pl.BlockSpec(memory_space=pltpu.VMEM)
     here = pl.BlockSpec(memory_space=pl.ANY)
@@ -402,11 +428,11 @@
         in_specs=[here, vmem, vmem] + [here] * 9,
         out_specs=here,
         scratch_shapes=[
-            pltpu.VMEM((4, 128, 128), F32),
+            pltpu.VMEM((16, 4, 8, 128), F32),
             pltpu.VMEM((2, 16, 4, 4, 8, 128), F32),
             pltpu.VMEM((2, 2, 256, 256), BF16),
-            pltpu.VMEM((2, 8, 4, 8, 8, 128), F32),
-            pltpu.VMEM((4, 8, 128, 128), F32),
+            pltpu.VMEM((2, 8, 8, 4, 8, 128), F32),
+            pltpu.VMEM((16, 8, 4, 8, 128), F32),
             pltpu.VMEM((2, 16, 1024), F32),
             pltpu.VMEM((16, 2, 256), F32),
             pltpu.VMEM((2, 512, 256), BF16),
@@ -420,9 +446,10 @@
             pltpu.VMEM((2, 16, 16, 128), F32),
             pltpu.VMEM((16, 16, 128), F32),
             pltpu.VMEM((16, 8, 128), F32),
-            pltpu.SemaphoreType.DMA((24,)),
-            pltpu.SemaphoreType.DMA((24,)),
-            pltpu.SemaphoreType.DMA((24,)),
+            pltpu.SemaphoreType.DMA((37,)),
+            pltpu.SemaphoreType.DMA((16,)),
+            pltpu.SemaphoreType.DMA((16,)),
+            pltpu.SemaphoreType.REGULAR,
         ],
         compiler_params=pltpu.CompilerParams(
             collective_id=0, has_side_effects=True, vmem_limit_bytes=60 << 20

time: 72.1 us -> 69.4 us (0.963)
  Pallas kernels: 70.5 us -> 67.7 us
    pallas_call x1, Pallas kernels: 70.5 us -> 67.7 us  [body(): pl.pallas_call(kernel, out_shape=jax.ShapeDtypeStruct((16, 8, 128), F32),...]
where the time goes in v4:
time: 69.4 us; the launch traced here: 69.2 us
  Pallas kernels  67.7 us (98%)
  local copies, waits for them, and re-layouts  1.47 us (2%)
    pallas_call x1, Pallas kernels, body(): pl.pallas_call(kernel, out_shape=jax.ShapeDtypeStruct((16, 8, 128), F32),...  67.7 us
    unnamed x1, local copies, waits for them, and re-layouts  1.47 us

profile of v4, /device:TPU:1, one launch (start us, length us, event | category | flops | bytes accessed | tf_op | source)
XLA Modules:
  0.0 69.2 jit_solution(408006281264093420)
XLA Ops:
  0.0 67.7 %shard_map.118 = f32[16,8,128]{2,1,0:T(8,128)} custom-call(f32[16,8,4,128]{3,2,1,0:T(4,128)} %bitcast.5, f32[8,256]{1,0:T(8,128)} %row_left_ref.1, f32[8,256]{1,0:T(8,128)} %row_right_ref.1, f32[8,16384]{1,0:T(8,128)} %left_ref.1, f32[8,16384]{1,0:T(8,128)} %right_ref.1, f32[256,2,256]{2,1,0:T(2,128)} %constant.14.clone.turn_hbm, ...), custom_call_target="tpu_custom_call" | custom-call | tf_op jit(solution)/shard_map/pallas_call | solution.py:425
  67.8 1.5 %copy.14 = f32[1,16384]{1,0:T(1,128)} copy(f32[1,16384]{1,0:T(1,128)} %bitcast.4) | data formatting | bytes 131072

commit v5 on v4

--- a/solution.py
+++ b/solution.py
@@ -14,7 +14,6 @@
 BF16 = jnp.bfloat16
 F32 = jnp.float32
 SIZE = {"x": 4, "y": 4, "z": 8}
-AHEAD = 4
 
 
 def halves(table):
@@ -100,7 +99,7 @@
     lines_ref, dense_ref, weight_ref, field_ref, all_ref, cols_ref,
     turn_ref, lead_ref, twist_ref, trail_ref, back_trail_ref, back_lead_ref, middle_ref,
     sum_ref, conv_ref, got_ref, part_ref, line_ref,
-    one_sem, send_sem, recv_sem, pair_sem,
+    one_sem, recv_sem, pair_sem,
 ):
     me = place()
     z, y, x, core = me["z"], me["y"], me["x"], me["core"]
@@ -129,9 +128,9 @@
     for row in range(4):
         pltpu.make_async_copy(d_ref.at[:, :, row], lines_ref.at[:, row], one_sem.at[0]).start()
     barrier = pltpu.get_barrier_semaphore()
-    friends = [at(z=z + o) for o in range(1, 8)]
+    friends = [at(z=z + o) for o in (2, 6, 1, 7)]
     friends += [at(y=y + o) for o in range(1, 4)]
-    friends += [at(x=x + o) for o in range(1, 4)]
+    friends += [at(x=x + o) for o in (1, 3)]
     friends += [at(core=1 - core)]
     for friend in friends:
         pl.semaphore_signal(barrier, inc=1, device_id=device(friend), device_id_type=MESH)
@@ -174,9 +173,6 @@
 
     pltpu.make_async_copy(lines_ref, lines_ref, one_sem.at[0]).wait()
     pl.semaphore_wait(barrier, len(friends))
-    pl.semaphore_signal(
-        pair_sem, inc=1, device_id=device(at(core=1 - core)), device_id_type=MESH
-    )
 
     def slices(region, where):
         return lines_ref.at[8 * region + group(region, where)]
@@ -194,7 +190,6 @@
     def await_block(block, sem):
         pltpu.make_async_copy(block, block, sem).wait()
 
-    near = [1, 7, 2, 6, 3, 5, 4]
     first_block = dense_ref.at[(0,) + mine]
     second_block = dense_ref.at[(1,) + mine]
     beside = at(x=x - 1 + z % 2 * 2)
@@ -202,49 +197,17 @@
     for o in range(1, 4):
         target = at(y=y + o)
         copy(slices(1, target), second_block, one_sem.at[2], one_sem.at[4], target)
-    for o in near:
-        copy(slices(0, me), first_block, one_sem.at[1], one_sem.at[24 + o], at(z=z + o))
     own = pltpu.make_async_copy(slices(0, me), first_block, one_sem.at[3])
     own.start()
     pltpu.make_async_copy(slices(1, me), second_block, one_sem.at[4]).start()
-    started = []
-
-    def send(block, target):
-        i = len(started)
-        copy = pltpu.make_async_remote_copy(
-            src_ref=block,
-            dst_ref=block,
-            send_sem=send_sem.at[i],
-            recv_sem=recv_sem.at[i],
-            device_id=device(target),
-            device_id_type=MESH,
-        )
-        copy.start()
-        started.append(copy)
-        return copy
-
-    def ring(axis, steps, block):
-        ahead = {1: [None, None], -1: [None, None]}
-        for step in range(1, steps + 1):
-            for turn in (0, 1):
-                for way in (1, -1):
-                    chunk = turn if way == 1 else 1 - turn
-                    if ahead[way][chunk] is not None:
-                        ahead[way][chunk].wait_recv()
-                        ahead[way][chunk] = None
-                    if step < steps or turn == 0:
-                        ahead[way][chunk] = send(
-                            block((me[axis] - way * (step - 1)) % SIZE[axis], chunk),
-                            at(**{axis: me[axis] + way}),
-                        )
-            yield
-        for way in (1, -1):
-            for copy in ahead[way]:
-                if copy is not None:
-                    copy.wait_recv()
-
-    def block_z(index, chunk):
-        return dense_ref.at[1, 2 * index + x % 2, pl.ds(2 * chunk, 2)]
+    def block_z(o, half=None):
+        index = (z + o) % 8 * 2 + x % 2
+        if half is None:
+            return dense_ref.at[1, index]
+        return dense_ref.at[1, index, pl.ds(2 * half, 2)]
+
+    def along_z(block, way, sem):
+        copy(block, block, one_sem.at[37], recv_sem.at[sem], at(z=z + way))
 
     def along_y(o):
         block = dense_ref.at[0, pl.ds((z - o) % 8 * 2, 2), y]
@@ -255,31 +218,55 @@
 
     def along_x(o):
         index = (z + o) % 8
-        block = dense_ref.at[1, 2 * index + x % 2]
+        block = block_z(o)
         copy(block, block, one_sem.at[34], one_sem.at[35], at(x=x + 1 - index % 2 * 2))
 
-    other_block = dense_ref.at[0, z * 2 + 1 - x % 2, y]
-    await_block(other_block, one_sem.at[24])
-    for o in near:
-        copy(other_block, other_block, one_sem.at[36], one_sem.at[24 + o], at(z=z + o))
+    def first_z(o):
+        block = dense_ref.at[0, pl.ds(2 * z, 2), y]
+        copy(block, block, one_sem.at[36], one_sem.at[24 + o], at(z=z + o))
+
+    await_block(dense_ref.at[1, z * 2 + x % 2], one_sem.at[4])
+    for sem, way in ((0, 2), (1, -2), (2, 1), (3, -1)):
+        along_z(block_z(0), way, sem)
+    along_x(0)
+    await_block(dense_ref.at[0, z * 2 + 1 - x % 2, y], one_sem.at[24])
     own.wait()
+    pl.semaphore_signal(
+        pair_sem, inc=1, device_id=device(at(core=1 - core)), device_id_type=MESH
+    )
+    first_z(1)
+    first_z(7)
     along_y(0)
-    await_block(dense_ref.at[1, z * 2 + x % 2], one_sem.at[4])
-    ring_z = ring("z", 4, block_z)
-    next(ring_z)
-    along_x(0)
-    for step in (1, 2, 3):
-        next(ring_z)
-        along_x(step)
-        along_x(-step)
-        along_y(step)
-        along_y(8 - step)
-    along_y(4)
-    for _ in ring_z:
-        pass
+    await_block(block_z(-2), recv_sem.at[0])
+    along_z(block_z(-2), 1, 4)
+    along_z(block_z(-2, 0), 2, 5)
+    await_block(block_z(2), recv_sem.at[1])
+    along_z(block_z(2), -1, 6)
+    along_z(block_z(2, 1), -2, 7)
+    first_z(2)
+    first_z(6)
+    await_block(block_z(-1), recv_sem.at[2])
+    await_block(block_z(1), recv_sem.at[3])
+    for o in (-1, 1, -2, 2):
+        along_x(o)
+    along_y(1)
+    along_y(7)
+    first_z(3)
+    first_z(5)
+    first_z(4)
+    along_y(2)
+    along_y(6)
+    await_block(block_z(-3), recv_sem.at[4])
+    along_x(-3)
+    await_block(block_z(3), recv_sem.at[6])
+    along_x(3)
+    await_block(block_z(4, 0), recv_sem.at[5])
+    await_block(block_z(4, 1), recv_sem.at[7])
     along_x(4)
-
-    counts = (1, 4)
+    for o in (3, 5, 4):
+        along_y(o)
+
+    counts = (1, 1)
 
     def region_fields(region):
         weights = (weight_ref[region, 0], weight_ref[region, 1])
@@ -349,18 +336,14 @@
     send_fields(0, 0)
     await_block(dense_ref.at[1, pl.ds(0, 8)], one_sem.at[35])
     region_fields(1)
-    for chunk in range(AHEAD):
-        send_fields(1, chunk)
+    send_fields(1, 0)
     sum_ref[...] = jnp.zeros_like(sum_ref)
     for target in (lead_ref, twist_ref, trail_ref, back_trail_ref, back_lead_ref, middle_ref):
         pltpu.make_async_copy(target, target, one_sem.at[9]).wait()
     arrived(0, 0)
-    for chunk in range(4):
-        arrived(1, chunk)
-        if chunk + AHEAD < 4:
-            send_fields(1, chunk + AHEAD)
-        convolve(2 * chunk)
-        convolve(2 * chunk + 1)
+    arrived(1, 0)
+    for r in range(8):
+        convolve(r)
 
     back = dot3(split(sum_ref[...]), table(back_trail_ref))
     real, imag = back[:, :128], back[:, 128:]
@@ -368,46 +351,46 @@
     turned = jnp.concatenate([real * cos + imag * sin, imag * cos - real * sin], axis=0)
     conv_ref[...] = dot3(table(back_lead_ref), split(turned)).reshape(16, 16, 128)
 
-    def by_i(i):
-        return at(z=i // 2, x=x // 2 * 2 + i % 2)
-
-    def by_j(j):
-        return at(y=j // 4, x=j % 4 // 2 * 2 + x % 2, core=j % 2)
-
-    def exchange(source, target, to, own, sems):
+    def others_i():
+        for dz in (4, 3, 5, 2, 6, 1, 7, 0):
+            for dx in (1, 0):
+                if dz or dx:
+                    to = at(z=z + dz, x=x // 2 * 2 + (x + dx) % 2)
+                    yield to["z"] * 2 + to["x"] % 2, to
+
+    def others_j():
+        for dy in (2, 1, 3, 0):
+            for dx in (2, 0):
+                for dc in (1, 0):
+                    if dy or dx or dc:
+                        to = at(y=y + dy, x=x + dx, core=(core + dc) % 2)
+                        yield to["y"] * 4 + to["x"] // 2 * 2 + to["core"], to
+
+    def exchange(source, target, others, own, sems):
+        for index, to in others():
+            copy(source.at[index], target.at[own], sems[0], sems[1], to)
         pltpu.make_async_copy(source.at[own], target.at[own], sems[1]).start()
-        for o in range(1, 16):
-            index = (own + o) % 16
-            pltpu.make_async_remote_copy(
-                src_ref=source.at[index],
-                dst_ref=target.at[own],
-                send_sem=sems[0],
-                recv_sem=sems[1],
-                device_id=device(to(index)),
-                device_id_type=MESH,
-            ).start()
         pltpu.make_async_copy(target, target, sems[1]).wait()
 
-    exchange(conv_ref, got_ref.at[0], by_i, mine_i, (one_sem.at[18], one_sem.at[19]))
+    exchange(conv_ref, got_ref.at[0], others_i, mine_i, (one_sem.at[18], one_sem.at[19]))
     values = [(got_ref[0, i, :8], got_ref[0, i, 8:]) for i in range(16)]
     for a, (real, imag) in enumerate(short_dft(values)):
         cos, sin = middle_ref[2 * a : 2 * a + 1], middle_ref[2 * a + 1 : 2 * a + 2]
         part_ref[a, :8] = real * cos - imag * sin
         part_ref[a, 8:] = real * sin + imag * cos
-    exchange(part_ref, got_ref.at[1], by_j, mine_j, (one_sem.at[20], one_sem.at[21]))
+    exchange(part_ref, got_ref.at[1], others_j, mine_j, (one_sem.at[20], one_sem.at[21]))
     values = [(got_ref[1, i, :8], got_ref[1, i, 8:]) for i in range(16)]
     for a, value in enumerate(short_dft(values)):
         line_ref[a] = scaled(value, a, 64)[0]
-    exchange(line_ref, out_ref, by_i, mine_i, (one_sem.at[22], one_sem.at[23]))
-
-    for copy in started:
-        copy.wait_send()
+    exchange(line_ref, out_ref, others_i, mine_i, (one_sem.at[22], one_sem.at[23]))
+
     for sent, sem in (
-        (dense_ref.at[0, pl.ds(0, 8), 0], 1),
+        (dense_ref.at[0, 0, 0], 1),
         (dense_ref.at[0, pl.ds(0, 3), 0], 2),
         (dense_ref.at[0, :, pl.ds(0, 3)], 32),
         (dense_ref.at[1, pl.ds(0, 8)], 34),
-        (dense_ref.at[0, pl.ds(0, 7), 0], 36),
+        (dense_ref.at[0, pl.ds(0, 14), 0], 36),
+        (dense_ref.at[1, pl.ds(0, 7)], 37),
     ):
         await_block(sent, one_sem.at[sem])
     sent = field_ref.at[:, pl.ds(0, 7)]
@@ -426,7 +409,7 @@
         kernel,
         out_shape=jax.ShapeDtypeStruct((16, 8, 128), F32),
         in_specs=[here, vmem, vmem] + [here] * 9,
-        out_specs=here,
+        out_specs=vmem,
         scratch_shapes=[
             pltpu.VMEM((16, 4, 8, 128), F32),
             pltpu.VMEM((2, 16, 4, 4, 8, 128), F32),
@@ -446,13 +429,12 @@
             pltpu.VMEM((2, 16, 16, 128), F32),
             pltpu.VMEM((16, 16, 128), F32),
             pltpu.VMEM((16, 8, 128), F32),
-            pltpu.SemaphoreType.DMA((37,)),
-            pltpu.SemaphoreType.DMA((16,)),
-            pltpu.SemaphoreType.DMA((16,)),
+            pltpu.SemaphoreType.DMA((38,)),
+            pltpu.SemaphoreType.DMA((8,)),
             pltpu.SemaphoreType.REGULAR,
         ],
         compiler_params=pltpu.CompilerParams(
-            collective_id=0, has_side_effects=True, vmem_limit_bytes=60 << 20
+            collective_id=0, has_side_effects=True, vmem_limit_bytes=55104 << 10
         ),
     )(lines, row_left, row_right, col_left, col_right, *constants)
     return out.reshape(1, 16384)

time: 69.4 us -> 66.8 us (0.963)
  Pallas kernels: 67.7 us -> 64.6 us
    pallas_call x1, Pallas kernels: 67.7 us -> 64.6 us  [body(): pl.pallas_call(kernel, out_shape=jax.ShapeDtypeStruct((16, 8, 128), F32),...]
    unnamed x1 -> x5, local copies, waits for them, and re-layouts: 1.47 us -> 2.02 us
where the time goes in v5:
time: 66.8 us; the launch traced here: 66.6 us
  Pallas kernels  64.6 us (97%)
  local copies, waits for them, and re-layouts  2.02 us (3%)
    pallas_call x1, Pallas kernels, body(): pl.pallas_call(kernel, out_shape=jax.ShapeDtypeStruct((16, 8, 128), F32),...  64.6 us
    unnamed x5, local copies, waits for them, and re-layouts  2.02 us

profile of v5, /device:TPU:1, one launch (start us, length us, event | category | flops | bytes accessed | tf_op | source)
XLA Modules:
  0.0 66.6 jit_solution(7802520457355563042)
XLA Ops:
  0.0 0.0 copy-start
  0.0 0.7 %copy-done = f32[8,256]{1,0:T(8,128)S(1)} copy-done((f32[8,256]{1,0:T(8,128)S(1)}, f32[8,256]{1,0:T(8,128)}, u32[]{:S(2)}) %copy-start) | copy-done | bytes 8216
  0.7 0.0 copy-start.1
  0.7 0.7 %copy-done.1 = f32[8,256]{1,0:T(8,128)S(1)} copy-done((f32[8,256]{1,0:T(8,128)S(1)}, f32[8,256]{1,0:T(8,128)}, u32[]{:S(2)}) %copy-start.1) | copy-done | bytes 8216
  1.4 64.6 %shard_map.118 = f32[16,8,128]{2,1,0:T(8,128)S(1)} custom-call(f32[16,8,4,128]{3,2,1,0:T(4,128)} %bitcast.5, f32[8,256]{1,0:T(8,128)S(1)} %copy-done, f32[8,256]{1,0:T(8,128)S(1)} %copy-done.1, f32[8,16384]{1,0:T(8,128)} %left_ref.1, f32[8,16384]{1,0:T(8,128)} %right_ref.1, f32[256,2,256]{2,1,0:T(2,128)} %constant.14.clone.turn_hbm, ...), custom_call_target="tpu_custom_call" | custom-call | tf_op jit(solution)/shard_map/pallas_call | solution.py:408
  66.0 0.6 copy.14
Async XLA Ops:
  0.0 0.7 %copy-start = (f32[8,256]{1,0:T(8,128)S(1)}, f32[8,256]{1,0:T(8,128)}, u32[]{:S(2)}) copy-start(f32[8,256]{1,0:T(8,128)} %row_left_ref.1) | copy-start | bytes 24580
  0.7 0.7 %copy-start.1 = (f32[8,256]{1,0:T(8,128)S(1)}, f32[8,256]{1,0:T(8,128)}, u32[]{:S(2)}) copy-start(f32[8,256]{1,0:T(8,128)} %row_right_ref.1) | copy-start | bytes 24580

commit v6 on v5

--- a/solution.py
+++ b/solution.py
@@ -330,13 +330,13 @@
         sum_ref[:, 128:] += lr * ri + li * rr
 
     pltpu.make_async_copy(cols_ref, cols_ref, one_sem.at[8]).wait()
+    await_block(dense_ref.at[1, pl.ds(0, 8)], one_sem.at[35])
+    pl.semaphore_wait(pair_sem, 1)
+    region_fields(1)
+    send_fields(1, 0)
     await_block(dense_ref.at[0, :, pl.ds(0, 3)], one_sem.at[33])
-    pl.semaphore_wait(pair_sem, 1)
     region_fields(0)
     send_fields(0, 0)
-    await_block(dense_ref.at[1, pl.ds(0, 8)], one_sem.at[35])
-    region_fields(1)
-    send_fields(1, 0)
     sum_ref[...] = jnp.zeros_like(sum_ref)
     for target in (lead_ref, twist_ref, trail_ref, back_trail_ref, back_lead_ref, middle_ref):
         pltpu.make_async_copy(target, target, one_sem.at[9]).wait()

time: 66.8 us -> 69.1 us (1.034)
  Pallas kernels: 64.6 us -> 66.9 us
    pallas_call x1, Pallas kernels: 64.6 us -> 66.9 us  [body(): pl.pallas_call(kernel, out_shape=jax.ShapeDtypeStruct((16, 8, 128), F32),...]
where the time goes in v6:
time: 69.1 us; the launch traced here: 68.9 us
  Pallas kernels  66.9 us (97%)
  local copies, waits for them, and re-layouts  2.02 us (3%)
    pallas_call x1, Pallas kernels, body(): pl.pallas_call(kernel, out_shape=jax.ShapeDtypeStruct((16, 8, 128), F32),...  66.9 us
    unnamed x5, local copies, waits for them, and re-layouts  2.02 us

profile of v6, /device:TPU:1, one launch (start us, length us, event | category | flops | bytes accessed | tf_op | source)
XLA Modules:
  0.0 68.9 jit_solution(1838676867055606638)
XLA Ops:
  0.0 0.0 copy-start
  0.0 0.7 %copy-done = f32[8,256]{1,0:T(8,128)S(1)} copy-done((f32[8,256]{1,0:T(8,128)S(1)}, f32[8,256]{1,0:T(8,128)}, u32[]{:S(2)}) %copy-start) | copy-done | bytes 8216
  0.7 0.0 copy-start.1
  0.7 0.7 %copy-done.1 = f32[8,256]{1,0:T(8,128)S(1)} copy-done((f32[8,256]{1,0:T(8,128)S(1)}, f32[8,256]{1,0:T(8,128)}, u32[]{:S(2)}) %copy-start.1) | copy-done | bytes 8216
  1.4 66.9 %shard_map.118 = f32[16,8,128]{2,1,0:T(8,128)S(1)} custom-call(f32[16,8,4,128]{3,2,1,0:T(4,128)} %bitcast.5, f32[8,256]{1,0:T(8,128)S(1)} %copy-done, f32[8,256]{1,0:T(8,128)S(1)} %copy-done.1, f32[8,16384]{1,0:T(8,128)} %left_ref.1, f32[8,16384]{1,0:T(8,128)} %right_ref.1, f32[256,2,256]{2,1,0:T(2,128)} %constant.14.clone.turn_hbm, ...), custom_call_target="tpu_custom_call" | custom-call | tf_op jit(solution)/shard_map/pallas_call | solution.py:408
  68.3 0.6 copy.14
Async XLA Ops:
  0.0 0.7 %copy-start = (f32[8,256]{1,0:T(8,128)S(1)}, f32[8,256]{1,0:T(8,128)}, u32[]{:S(2)}) copy-start(f32[8,256]{1,0:T(8,128)} %row_left_ref.1) | copy-start | bytes 24580
  0.7 0.7 %copy-start.1 = (f32[8,256]{1,0:T(8,128)S(1)}, f32[8,256]{1,0:T(8,128)}, u32[]{:S(2)}) copy-start(f32[8,256]{1,0:T(8,128)} %row_right_ref.1) | copy-start | bytes 24580
